TPU v7x, 32 devices: a whole 2x2x4 slice. The times are simulated.
32 devices in a mesh: section: 4 (over y, x), expert: 8 (over z, core).
Axes of the slice: x: 2, y: 2, z: 4, core: 2. Of those that a mesh axis runs over, the one named last changes fastest.
Arguments:
- tokens: bfloat16 [4, 2, 512, 2048], P('section', None, 'expert'), may hold values from -6 to 6
- routes: int32 [4, 1, 2, 512, 2], P('section', None, None, 'expert'), may hold values from 0 to 7, all different within a row; in each aligned block of 64 rows (0 to 63, 64 to 127, ..., all dimensions but the last counted through in order) at most 20 rows name the same one
- norm_gain: bfloat16 [4, 2048], P('section'), may hold values from 0.5 to 1.5
- router: bfloat16 [4, 2048, 8], P('section')
- gate_weight: bfloat16 [4, 2048, 8192], P('section', None, 'expert'), may hold values from -0.125 to 0.125
- up_weight: bfloat16 [4, 2048, 8192], P('section', None, 'expert'), may hold values from -0.125 to 0.125
- down_weight: bfloat16 [4, 8192, 2048], P('section', 'expert'), may hold values from -0.1875 to 0.1875
Outputs:
- mixed: bfloat16 [4, 2, 512, 2048], P('section', None, 'expert')
Inputs may be any that keep to these rules, and one draw needn't show every extreme that they name: `routes`: each token names 2 different experts. Within the 64 rows of one device for one start section, layer step and micro-batch, no expert is named more than 20 times, a bound that some block reaches.
All inputs are finite; a program needn't handle non-finite values.
Results may differ from a plain program's by a relative error of at most 0.0045.
Values may be sent and summed in bfloat16 or wider, within the bound.
No kernel may reach another device: no remote copies, remote signals or barrier semaphores. Data moves between devices by JAX's collectives and lax.ppermute only.
A program may use at most 128 MiB of HBM per device.

v0:
```python
import jax
import jax.numpy as jnp
from jax import lax
from jax.sharding import PartitionSpec as P

ROUNDS = 1
CAP = 20


epsilon = 1e-06


def passed_along(shard, axis, by):
    length = lax.axis_size(axis)
    return lax.ppermute(shard, axis, [(i, (i + by) % length) for i in range(length)])


def prepare(current, routing, norm_gain, router, capacity, groups):
    experts = router.shape[1]
    features = current.shape[1]
    wide_rows = current.astype(jnp.float32)
    normed = (
        wide_rows
        * lax.rsqrt(jnp.mean(wide_rows * wide_rows, axis=-1, keepdims=True) + epsilon)
        * norm_gain.astype(jnp.float32)
    ).astype(jnp.bfloat16)
    logits = jnp.dot(normed, router, preferred_element_type=jnp.float32)
    chosen = jnp.take_along_axis(logits, routing, axis=1)
    route_weight = jax.nn.softmax(chosen, axis=-1)
    matches = jnp.any(
        routing[:, :, None] == jnp.arange(experts, dtype=jnp.int32)[None, None, :], axis=1
    )
    running = jnp.cumsum(matches.astype(jnp.int32), axis=0) - 1
    slot_index = jnp.take_along_axis(running, routing, axis=1)
    flat_slot = routing * capacity + slot_index
    slot_ids = jnp.arange(experts * capacity, dtype=jnp.int32)
    selector = jnp.any(flat_slot[None, :, :] == slot_ids[:, None, None], axis=2).astype(
        jnp.bfloat16
    )
    packed = jnp.dot(selector, normed, preferred_element_type=jnp.float32).astype(jnp.bfloat16)
    packed = packed.reshape(experts, 1, capacity, features)
    outgoing = jnp.broadcast_to(packed, (experts, groups, capacity, features)).reshape(
        experts * groups, capacity, features
    )
    return (outgoing, flat_slot, route_weight, wide_rows)


def expert_apply(received, gate_weight, up_weight, down_weight):
    sources, slots, features = received.shape
    flat_rows = received.reshape(sources * slots, features)
    gate_act = jnp.dot(flat_rows, gate_weight, preferred_element_type=jnp.float32)
    up_act = jnp.dot(flat_rows, up_weight, preferred_element_type=jnp.float32)
    hidden = (jax.nn.silu(gate_act) * up_act).astype(jnp.bfloat16)
    partial_value = jnp.dot(hidden, down_weight, preferred_element_type=jnp.float32).astype(
        jnp.bfloat16
    )
    return partial_value.reshape(sources, slots, features)


def finish(returned, flat_slot, route_weight, wide_rows, experts, groups, capacity):
    features = returned.shape[2]
    summed = returned.reshape(experts, groups, capacity, features).astype(jnp.float32).sum(axis=1)
    summed = summed.reshape(experts * capacity, features)
    picked = jnp.take(summed, flat_slot, axis=0)
    added = jnp.sum(route_weight[:, :, None] * picked, axis=1)
    return (wide_rows + added).astype(jnp.bfloat16)


def run_layer(current, routing, params, capacity, groups):
    norm_gain, router, gate_weight, up_weight, down_weight = params
    experts = router.shape[1]
    batches = current.shape[0]
    prepared = [
        prepare(current[batch_index], routing[batch_index], norm_gain, router, capacity, groups)
        for batch_index in range(batches)
    ]
    outgoing = jnp.concatenate([bundle[0] for bundle in prepared], axis=1)
    returned = lax.all_to_all(
        expert_apply(
            lax.all_to_all(outgoing, "expert", split_axis=0, concat_axis=0, tiled=True),
            gate_weight,
            up_weight,
            down_weight,
        ),
        "expert",
        split_axis=0,
        concat_axis=0,
        tiled=True,
    )
    pieces = [
        returned[:, batch_index * capacity : (batch_index + 1) * capacity]
        for batch_index in range(batches)
    ]
    results = [
        finish(
            pieces[batch_index],
            prepared[batch_index][1],
            prepared[batch_index][2],
            prepared[batch_index][3],
            experts,
            groups,
            capacity,
        )
        for batch_index in range(batches)
    ]
    return jnp.stack(results)


def shards(tokens, routes, norm_gain, router, gate_weight, up_weight, down_weight):
    experts = router.shape[2]
    groups = lax.axis_size("expert") // experts
    capacity = CAP
    current = tokens[0]
    routing = routes[0]
    params = (norm_gain[0], router[0], gate_weight[0], up_weight[0], down_weight[0])
    current, routing = passed_along((current, routing), "section", 1)
    current = run_layer(current, routing[0], params, capacity, groups)
    current = passed_along(current, "section", -ROUNDS)
    return current[None]


def solution(mesh):
    placed = (
        P("section", None, "expert", None),
        P("section", None, None, "expert", None),
        P("section", None),
        P("section", None, None),
        P("section", None, "expert"),
        P("section", None, "expert"),
        P("section", "expert", None),
    )
    return jax.shard_map(
        shards,
        mesh=mesh,
        in_specs=placed,
        out_specs=P("section", None, "expert", None),
        check_vma=False,
    )
```

profile of v0, /device:TPU:0, one launch (start us, length us, event | category | flops | bytes accessed | tf_op | source)
XLA Modules:
  0.0 135.8 jit_solution(14544167632067014855)
XLA Ops:
  0.0 2.9 %collective-permute-start.1 = (s32[1,2,64,2]{2,3,1,0:T(2,128)}, s32[1,2,64,2]{2,3,1,0:T(2,128)S(1)}, u32[]{:S(2)}, u32[]{:S(2)}) collective-permute-start(s32[1,2,64,2]{2,3,1,0:T(2,128)} %bitcast.106), channel_id=1, source_target_pairs={{0,8},{8,16},{16,24},{24,0},{1,9},{9,17},{17,25},{25,1},{2,10},{10... | collective-permute-start | bytes 3080 | tf_op jit(solution)/shard_map/ppermute | solution.py:15
  2.9 1.5 %collective-permute-start = (bf16[2,64,2048]{2,1,0:T(8,128)(2,1)}, bf16[2,64,2048]{2,1,0:T(8,128)(2,1)S(1)}, u32[]{:S(2)}, u32[]{:S(2)}) collective-permute-start(bf16[2,64,2048]{2,1,0:T(8,128)(2,1)} %bitcast.105), channel_id=1, source_target_pairs={{0,8},{8,16},{16,24},{24,0},{1,9},{9,17},{17,25},{25,1},{2,10},{10... | collective-permute-start | bytes 1572872 | tf_op jit(solution)/shard_map/ppermute | solution.py:15
  4.4 0.7 mul.113
  5.1 0.5 collective-permute-done.1
  6.0 0.1 reshape.196
  6.4 1.3 gather_fusion.1
  8.1 1.3 gather_fusion.2
  9.6 7.9 %collective-permute-done = bf16[2,64,2048]{2,1,0:T(8,128)(2,1)S(1)} collective-permute-done((bf16[2,64,2048]{2,1,0:T(8,128)(2,1)}, bf16[2,64,2048]{2,1,0:T(8,128)(2,1)S(1)}, u32[]{:S(2)}, u32[]{:S(2)}) %collective-permute-start) | collective-permute-done | bytes 524320 | tf_op jit(solution)/shard_map/ppermute | solution.py:15
  17.4 0.2 fusion.27
  17.7 0.2 fusion.37
  17.9 1.0 gather_fusion.4
  19.1 0.3 fusion.40
  19.4 1.0 gather_fusion
  20.8 0.4 convolution_convert_fusion.1
  21.4 0.4 convolution_convert_fusion
  22.0 0.3 pad_maximum_fusion
  22.3 37.2 %all_to_all.10 = bf16[8,40,2048]{2,1,0:T(8,128)(2,1)S(1)} all-to-all(bf16[8,40,2048]{2,1,0:T(8,128)(2,1)S(1)} %pad_maximum_fusion), channel_id=1, replica_groups=mesh['section'=4,'expert'=8] {'expert'}, dimensions={0} | all-to-all | bytes 2621440 | tf_op jit(solution)/shard_map/all_to_all | solution.py:80
  59.4 2.6 %fusion.4 = f32[320,1024]{1,0:T(8,128)} fusion(bf16[320,2048]{1,0:T(8,128)(2,1)S(1)} %bitcast.98, bf16[1,2048,1024]{2,1,0:T(8,128)(2,1)S(1)} %copy-done.3), kind=kOutput, calls=%fused_computation.10 | convolution fusion | flops 1342177280 | bytes 6815744 | tf_op jit(solution)/shard_map/dot_general | solution.py:51
  62.1 7.9 %fusion.6 = bf16[320,2048]{1,0:T(8,128)(2,1)} fusion(bf16[1,1024,2048]{2,1,0:T(8,128)(2,1)} %param.19, bf16[320,2048]{1,0:T(8,128)(2,1)S(1)} %bitcast.99, bf16[1,2048,1024]{2,1,0:T(8,128)(2,1)} %param.18, f32[320,1024]{1,0:T(8,128)} %fusion.4), kind=kOutput, calls=%fused_computation.12 | convolution fusion | flops 2686976000 | bytes 12320768 | tf_op jit(solution)/shard_map/dot_general | solution.py:54
  69.9 3.7 %all-to-all-start.1 = ((bf16[8,40,2048]{2,1,0:T(8,128)(2,1)}), bf16[8,40,2048]{2,1,0:T(8,128)(2,1)S(1)}, u32[]{:S(2)}, u32[]{:S(2)}) async-start(bf16[8,40,2048]{2,1,0:T(8,128)(2,1)} %bitcast.16), calls=%async_computation.1 | async-start | bytes 2621440 | tf_op jit(solution)/shard_map/all_to_all | solution.py:78
  74.7 30.9 %all-to-all-done.1 = bf16[8,40,2048]{2,1,0:T(8,128)(2,1)S(1)} async-done(((bf16[8,40,2048]{2,1,0:T(8,128)(2,1)}), bf16[8,40,2048]{2,1,0:T(8,128)(2,1)S(1)}, u32[]{:S(2)}, u32[]{:S(2)}) %all-to-all-start.1) | async-done | bytes 1310752 | tf_op jit(solution)/shard_map/all_to_all | solution.py:78
  105.7 1.5 %slice_convert_fusion.1 = (f32[8,20,2048]{2,1,0:T(8,128)S(1)}, f32[8,20,2048]{2,1,0:T(8,128)}) fusion(bf16[8,40,2048]{2,1,0:T(8,128)(2,1)S(1)} %all-to-all-done.1), kind=kLoop, calls=%fused_computation.23 | loop fusion | flops 655360 | bytes 3932160 | tf_op jit(solution)/shard_map/reshape | solution.py:63
  107.2 1.5 %reshape.130 = f32[160,2048]{1,0:T(8,128)S(1)} reshape(f32[8,20,2048]{2,1,0:T(8,128)} %get-tuple-element.19) | data formatting | bytes 2621440 | tf_op jit(solution)/shard_map/reshape | solution.py:63
  108.6 2.0 %gather_fusion.5 = f32[128,2048]{1,0:T(8,128)} fusion(f32[160,2048]{1,0:T(8,128)S(1)} %reshape.130, s32[1024]{0:T(1024)S(1)} %pad_clamp_fusion), kind=kCustom, calls=%fused_computation.5.clone | custom fusion | bytes 2097664 | tf_op jit(solution)/shard_map/jit(_take)/gather | solution.py:64
  110.6 2.8 %reshape.222 = f32[64,2,2048]{2,1,0:T(2,128)} reshape(f32[128,2048]{1,0:T(8,128)} %gather_fusion.5) | data formatting | bytes 2097152 | tf_op jit(solution)/shard_map/jit(_take)/gather | solution.py:64
  113.6 1.0 gather_fusion.3
  114.6 1.7 %reshape.213 = f32[64,2,2048]{2,1,0:T(2,128)} reshape(f32[128,2048]{1,0:T(8,128)S(1)} %gather_fusion.3) | data formatting | bytes 2097152 | tf_op jit(solution)/shard_map/jit(_take)/gather | solution.py:64
  116.3 2.5 %fusion.15 = f32[64,2048]{1,0:T(8,128)S(1)} fusion(f32[64,2,2048]{2,1,0:T(2,128)S(1)} %copy-done.1, pred[64,2]{1,0:T(8,128)(4,1)S(1)} %copy.58, f32[64,2]{1,0:T(8,128)S(1)} %copy.57), kind=kLoop, calls=%fused_computation.19 | loop fusion | flops 655360 | bytes 1573504 | tf_op jit(solution)/shard_map/reduce_sum | solution.py:65
  118.8 2.5 %fusion.16 = f32[64,2048]{1,0:T(8,128)S(1)} fusion(f32[64,2,2048]{2,1,0:T(2,128)S(1)} %copy-done.2, pred[64,2]{1,0:T(8,128)(4,1)S(1)} %copy.50, f32[64,2]{1,0:T(8,128)S(1)} %copy.46), kind=kLoop, calls=%fused_computation.21 | loop fusion | flops 655360 | bytes 1573504 | tf_op jit(solution)/shard_map/reduce_sum | solution.py:65
  121.5 0.6 collective-permute-start.2
  122.1 12.9 %collective-permute-done.2 = bf16[2,64,2048]{2,1,0:T(8,128)(2,1)S(1)} collective-permute-done((bf16[2,64,2048]{2,1,0:T(8,128)(2,1)S(1)}, bf16[2,64,2048]{2,1,0:T(8,128)(2,1)S(1)}, u32[]{:S(2)}, u32[]{:S(2)}) %collective-permute-start.2) | collective-permute-done | bytes 524320 | tf_op jit(solution)/shard_map/ppermute | solution.py:15
  135.1 0.8 copy.61
  (56 shorter events, 3.4 us)
Async XLA Ops:
  0.0 17.7 %copy-start = (bf16[1,2048,8]{1,2,0:T(8,128)(2,1)S(1)}, bf16[1,2048,8]{1,2,0:T(8,128)(2,1)}, u32[]{:S(2)}) copy-start(bf16[1,2048,8]{1,2,0:T(8,128)(2,1)} %param.16) | copy-start | bytes 98308
  0.0 5.7 %collective-permute-start.1 = (s32[1,2,64,2]{2,3,1,0:T(2,128)}, s32[1,2,64,2]{2,3,1,0:T(2,128)S(1)}, u32[]{:S(2)}, u32[]{:S(2)}) collective-permute-start(s32[1,2,64,2]{2,3,1,0:T(2,128)} %bitcast.106), channel_id=1, source_target_pairs={{0,8},{8,16},{16,24},{24,0},{1,9},{9,17},{17,25},{25,1},{2,10},{10... | collective-permute-start | bytes 3080 | tf_op jit(solution)/shard_map/ppermute | solution.py:15
  2.9 14.5 %collective-permute-start = (bf16[2,64,2048]{2,1,0:T(8,128)(2,1)}, bf16[2,64,2048]{2,1,0:T(8,128)(2,1)S(1)}, u32[]{:S(2)}, u32[]{:S(2)}) collective-permute-start(bf16[2,64,2048]{2,1,0:T(8,128)(2,1)} %bitcast.105), channel_id=1, source_target_pairs={{0,8},{8,16},{16,24},{24,0},{1,9},{9,17},{17,25},{25,1},{2,10},{10... | collective-permute-start | bytes 1572872 | tf_op jit(solution)/shard_map/ppermute | solution.py:15
  22.0 37.4 %copy-start.3 = (bf16[1,2048,1024]{2,1,0:T(8,128)(2,1)S(1)}, bf16[1,2048,1024]{2,1,0:T(8,128)(2,1)}, u32[]{:S(2)}) copy-start(bf16[1,2048,1024]{2,1,0:T(8,128)(2,1)} %param.17) | copy-start | bytes 12582916
  69.9 35.7 %all-to-all-start.1 = ((bf16[8,40,2048]{2,1,0:T(8,128)(2,1)}), bf16[8,40,2048]{2,1,0:T(8,128)(2,1)S(1)}, u32[]{:S(2)}, u32[]{:S(2)}) async-start(bf16[8,40,2048]{2,1,0:T(8,128)(2,1)} %bitcast.16), calls=%async_computation.1 | async-start | bytes 2621440 | tf_op jit(solution)/shard_map/all_to_all | solution.py:78
  114.6 1.7 %copy-start.1 = (f32[64,2,2048]{2,1,0:T(2,128)S(1)}, f32[64,2,2048]{2,1,0:T(2,128)}, u32[]{:S(2)}) copy-start(f32[64,2,2048]{2,1,0:T(2,128)} %reshape.222) | copy-start | bytes 3145732
  116.3 2.5 %copy-start.2 = (f32[64,2,2048]{2,1,0:T(2,128)S(1)}, f32[64,2,2048]{2,1,0:T(2,128)}, u32[]{:S(2)}) copy-start(f32[64,2,2048]{2,1,0:T(2,128)} %reshape.213) | copy-start | bytes 3145732
  121.5 13.5 %collective-permute-start.2 = (bf16[2,64,2048]{2,1,0:T(8,128)(2,1)S(1)}, bf16[2,64,2048]{2,1,0:T(8,128)(2,1)S(1)}, u32[]{:S(2)}, u32[]{:S(2)}) collective-permute-start(bf16[2,64,2048]{2,1,0:T(8,128)(2,1)S(1)} %pad_maximum_fusion.1), channel_id=1, source_target_pairs={{0,24},{8,0},{16,8},{24,16},{1,25},{9,1},{17,9},{25,17},{2,26},{10... | collective-permute-start | bytes 1572872 | tf_op jit(solution)/shard_map/ppermute | solution.py:15
where the time goes:
time: 136 us
  waiting for transfers between devices  52.2 us (38%)
  blocking collectives  37.2 us (27%)
  local copies, waits for them, and re-layouts  17 us (12%)
  matrix products  11.8 us (9%)
  starting transfers between devices  8.79 us (6%)
  other arithmetic  8.5 us (6%)
    all_to_all x1, blocking collectives, run_layer(): lax.all_to_all(outgoing, 'expert', split_axis=0, concat_axis=0, tiled=True)  37.2 us
    all_to_all x1, waiting for transfers between devices, run_layer(): lax.all_to_all(expert_apply(lax.all_to_all(outgoing, 'expert', split_axis...  30.9 us
    ppermute x3, waiting for transfers between devices, passed_along(): lax.ppermute(shard, axis, [(i, (i + by) % length) for i in range(length)])  21.3 us
    dot_general x1, matrix products, expert_apply(): jnp.dot(hidden, down_weight, preferred_element_type=jnp.float32)  7.89 us
    gather x4, local copies, waits for them, and re-layouts, finish(): picked = jnp.take(summed, flat_slot, axis=0)  7.44 us
    reduce_sum x2, other arithmetic, finish(): added = jnp.sum(route_weight[:, :, None] * picked, axis=1)  5.05 us
    ppermute x3, starting transfers between devices, passed_along(): lax.ppermute(shard, axis, [(i, (i + by) % length) for i in range(length)])  5.04 us
    all_to_all x1, starting transfers between devices, run_layer(): lax.all_to_all(expert_apply(lax.all_to_all(outgoing, 'expert', split_axis...  3.75 us
  transfers between devices with their start and end apart: 4, of which 4 were waited for; matrix products, arithmetic and copies ran while one was open for 4% of the time, Pallas kernels for 0%

commit v1 on v0

v1 whole, which is shorter than its diff:
```python
import functools

import jax
import jax.numpy as jnp
from jax import lax
from jax.experimental import pallas as pl
from jax.experimental.pallas import tpu as pltpu
from jax.sharding import PartitionSpec as P

CAP = 20
FIRST = 16
epsilon = 1e-06
HOME = ("section", "expert")


def moved(block, by, flip):
    sections, width = lax.axis_size("section"), lax.axis_size("expert")
    pairs = [
        (s * width + e, (s + by) % sections * width + (e ^ flip))
        for s in range(sections)
        for e in range(width)
    ]
    return lax.ppermute(block, HOME, pairs)


def ranks(me, chosen, width, groups):
    tokens = chosen.shape[1]
    owner = lax.broadcasted_iota(jnp.int32, (width, tokens), 0) ^ me
    expert = owner // groups if groups > 1 else owner
    first = chosen[0:1, :] == expert
    match = first | (chosen[1:2, :] == expert)
    before = lax.broadcasted_iota(jnp.int32, (tokens, tokens), 0) < lax.broadcasted_iota(
        jnp.int32, (tokens, tokens), 1
    )
    rank = jnp.dot(
        match.astype(jnp.bfloat16), before.astype(jnp.bfloat16), preferred_element_type=jnp.float32
    ).astype(jnp.int32)
    return first, jnp.where(match, rank, -1)


def slots_of(rank, start, size):
    width, tokens = rank.shape
    place = lax.broadcasted_iota(jnp.int32, (width, size, tokens), 1) + start
    return rank[:, None, :] == place


def pack_kernel(width, groups, parts, me_ref, chosen_ref, rows_ref, *out_refs):
    _, rank = ranks(me_ref[0], chosen_ref[...], width, groups)
    rows = rows_ref[...]
    half = width // 2
    for part, (start, size) in enumerate(parts):
        select = slots_of(rank, start, size).astype(jnp.float32)
        select = select.reshape(width * size, rows.shape[0]).astype(jnp.bfloat16)
        for j in range(half):
            block = select[2 * j * size : 2 * (j + 1) * size]
            out_refs[part * half + j][...] = jnp.dot(
                block, rows, preferred_element_type=jnp.float32
            ).astype(jnp.bfloat16)


def weight_kernel(width, groups, parts, me_ref, chosen_ref, rows_ref, gain_ref, router_ref, *out_refs):
    chosen = chosen_ref[...]
    first, rank = ranks(me_ref[0], chosen, width, groups)
    normed = normalised(rows_ref[...], gain_ref[...])
    logits = lax.dot_general(
        router_ref[...], normed, (((1,), (1,)), ((), ())), preferred_element_type=jnp.float32
    )
    names = lax.broadcasted_iota(jnp.int32, logits.shape, 0)
    one = jnp.sum(jnp.where(names == chosen[0:1, :], logits, 0.0), axis=0, keepdims=True)
    two = jnp.sum(jnp.where(names == chosen[1:2, :], logits, 0.0), axis=0, keepdims=True)
    top = jnp.maximum(one, two)
    one, two = jnp.exp(one - top), jnp.exp(two - top)
    total = one + two
    weight = jnp.where(first, one / total, two / total)
    for part, (start, size) in enumerate(parts):
        wide = jnp.where(slots_of(rank, start, size), weight[:, None, :], 0.0)
        wide = wide.reshape(width * size, weight.shape[1])
        high = wide.astype(jnp.bfloat16)
        out_refs[part][0] = high
        out_refs[part][1] = (wide - high.astype(jnp.float32)).astype(jnp.bfloat16)


def normalised(rows, gain):
    wide = rows.astype(jnp.float32)
    scale = lax.rsqrt(jnp.mean(wide * wide, axis=-1, keepdims=True) + epsilon)
    return (wide * scale * gain.astype(jnp.float32)).astype(jnp.bfloat16)


def expert_kernel(half, size, steps, *refs):
    blocks, (passed_ref, gain_ref, gate_ref, up_ref, down_ref) = refs[:half], refs[half : half + 5]
    keep_ref, give_ref, normed_ref, total_ref = refs[half + 5 :]
    step = pl.program_id(0)

    @pl.when(step == 0)
    def _():
        gain = gain_ref[...]
        for j in range(half):
            normed_ref[j * size : (j + 1) * size] = normalised(blocks[j][0:size], gain)
        normed_ref[half * size :] = normalised(passed_ref[...], gain)

    normed = normed_ref[...]
    gate = jnp.dot(normed, gate_ref[...], preferred_element_type=jnp.float32)
    up = jnp.dot(normed, up_ref[...], preferred_element_type=jnp.float32)
    hidden = (gate / (1.0 + jnp.exp(-gate)) * up).astype(jnp.bfloat16)
    share = jnp.dot(hidden, down_ref[...], preferred_element_type=jnp.float32)

    @pl.when(step == 0)
    def _():
        total_ref[...] = share

    @pl.when(step > 0)
    def _():
        total_ref[...] += share

    @pl.when(step == steps - 1)
    def _():
        keep_ref[...] = total_ref[0 : half * size].astype(jnp.bfloat16)
        give_ref[...] = total_ref[half * size :].astype(jnp.bfloat16)


def combine_kernel(sizes, half, rows_ref, *refs):
    weights, blocks, out_ref = refs[: len(sizes)], refs[len(sizes) : -1], refs[-1]
    total = rows_ref[...].astype(jnp.float32)
    for part, size in enumerate(sizes):
        values = jnp.concatenate([ref[...] for ref in blocks[part * half : (part + 1) * half]], axis=0)
        for term in range(2):
            total += jnp.dot(weights[part][term], values, preferred_element_type=jnp.float32)
    out_ref[...] = total.astype(jnp.bfloat16)


SMEM = pl.BlockSpec(memory_space=pltpu.SMEM)
VMEM = pl.BlockSpec(memory_space=pltpu.VMEM)
LIMIT = 40 * 1024 * 1024


def run_experts(blocks, passed, size, gain, gate, up, down):
    half, features = len(blocks), gain.shape[1]
    rows, units = 2 * half * size, gate.shape[1]
    tile = min(256, units)
    steps = units // tile
    fixed = lambda shape: pl.BlockSpec(shape, lambda i: (0, 0))
    part = jax.ShapeDtypeStruct((half * size, features), jnp.bfloat16)
    return pl.pallas_call(
        functools.partial(expert_kernel, half, size, steps),
        grid=(steps,),
        in_specs=[fixed((2 * size, features))] * half
        + [
            fixed((half * size, features)),
            fixed((1, features)),
            pl.BlockSpec((features, tile), lambda i: (0, i)),
            pl.BlockSpec((features, tile), lambda i: (0, i)),
            pl.BlockSpec((tile, features), lambda i: (i, 0)),
        ],
        out_specs=[fixed((half * size, features))] * 2,
        out_shape=[part, part],
        scratch_shapes=[
            pltpu.VMEM((rows, features), jnp.bfloat16),
            pltpu.VMEM((rows, features), jnp.float32),
        ],
        compiler_params=pltpu.CompilerParams(vmem_limit_bytes=LIMIT),
        cost_estimate=pl.CostEstimate(
            flops=6 * rows * features * units,
            bytes_accessed=6 * features * units + 8 * rows * features,
            transcendentals=rows * units,
        ),
        name="experts",
    )(*blocks, passed, gain, gate, up, down)


def shards(tokens, routes, norm_gain, router, gate_weight, up_weight, down_weight):
    batches, count, features = tokens.shape[1:]
    experts = router.shape[2]
    width = lax.axis_size("expert")
    groups, half = width // experts, width // 2
    parts = ((0, FIRST), (FIRST, batches * CAP - FIRST))
    rows = tokens.reshape(batches * count, features)
    chosen = routes.reshape(batches * count, 2).T
    me = lax.axis_index("expert").astype(jnp.int32).reshape(1)

    outgoing = pl.pallas_call(
        functools.partial(pack_kernel, width, groups, parts),
        in_specs=[SMEM, VMEM, VMEM],
        out_specs=[VMEM] * (2 * half),
        out_shape=[
            jax.ShapeDtypeStruct((2 * size, features), jnp.bfloat16)
            for _, size in parts
            for _ in range(half)
        ],
        compiler_params=pltpu.CompilerParams(vmem_limit_bytes=LIMIT),
        name="pack",
    )(me, chosen, rows)

    far_first = range(half - 1, -1, -1)
    returned = []
    arrived = []
    for part in range(len(parts)):
        got = {j: moved(outgoing[part * half + j], 1, 2 * j) for j in far_first}
        arrived.append([got[j] for j in range(half)])

    gain_there = moved(norm_gain, -1, 0)
    router_there = moved(router[0].T, -1, 0)
    weights = pl.pallas_call(
        functools.partial(weight_kernel, width, groups, parts),
        in_specs=[SMEM, VMEM, VMEM, VMEM, VMEM],
        out_specs=[VMEM] * 2,
        out_shape=[
            jax.ShapeDtypeStruct((2, width * size, batches * count), jnp.bfloat16)
            for _, size in parts
        ],
        compiler_params=pltpu.CompilerParams(vmem_limit_bytes=LIMIT),
        name="weights",
    )(me, chosen, rows, gain_there, router_there)
    weights = [jnp.swapaxes(weight, 1, 2) for weight in weights]

    for part, (_, size) in enumerate(parts):
        blocks = arrived[part]
        passed = moved(jnp.concatenate([block[size:] for block in blocks], axis=0), 0, 1)
        keep, give = run_experts(
            blocks, passed, size, norm_gain, gate_weight[0], up_weight[0], down_weight[0]
        )
        taken = moved(give, 0, 1)
        both = [
            jnp.concatenate([keep[j * size : (j + 1) * size], taken[j * size : (j + 1) * size]], axis=0)
            for j in range(half)
        ]
        got = {j: moved(both[j], -1, 2 * j) for j in far_first}
        returned += [got[j] for j in range(half)]

    columns = min(512, features)
    mixed = pl.pallas_call(
        functools.partial(combine_kernel, [size for _, size in parts], half),
        grid=(features // columns,),
        in_specs=[pl.BlockSpec((batches * count, columns), lambda i: (0, i))]
        + [pl.BlockSpec(weight.shape, lambda i: (0, 0, 0)) for weight in weights]
        + [pl.BlockSpec((block.shape[0], columns), lambda i: (0, i)) for block in returned],
        out_specs=pl.BlockSpec((batches * count, columns), lambda i: (0, i)),
        out_shape=jax.ShapeDtypeStruct(rows.shape, jnp.bfloat16),
        compiler_params=pltpu.CompilerParams(vmem_limit_bytes=LIMIT),
        name="combine",
    )(rows, *weights, *returned)
    return mixed.reshape(tokens.shape)


def solution(mesh):
    placed = (
        P("section", None, "expert", None),
        P("section", None, None, "expert", None),
        P("section", None),
        P("section", None, None),
        P("section", None, "expert"),
        P("section", None, "expert"),
        P("section", "expert", None),
    )
    return jax.shard_map(
        shards,
        mesh=mesh,
        in_specs=placed,
        out_specs=P("section", None, "expert", None),
        check_vma=False,
    )
```

time: 136 us -> 104 us (0.76)
  starting transfers between devices: 8.79 us -> 49.6 us
  blocking collectives: 37.2 us -> 0 us
  waiting for transfers between devices: 52.2 us -> 27.3 us
  Pallas kernels: 0 us -> 14 us
  matrix products: 11.8 us -> 0 us
  other arithmetic: 8.5 us -> 0.15 us
  local copies, waits for them, and re-layouts: 17 us -> 11.6 us
    ppermute x3 -> x22, starting transfers between devices: 5.04 us -> 49.6 us  [moved(): return lax.ppermute(block, HOME, pairs)]
    all_to_all x1 -> x0, blocking collectives: 37.2 us -> none  [run_layer(): lax.all_to_all(outgoing, 'expert', split_axis=0, concat_axis=0, tiled=True)]
    all_to_all x1 -> x0, waiting for transfers between devices: 30.9 us -> none  [run_layer(): lax.all_to_all(expert_apply(lax.all_to_all(outgoing, 'expert', split_axis...]
    pallas_call x0 -> x5, Pallas kernels: none -> 14 us  [the longest x2 10.4 us: run_experts(): pl.pallas_call(functools.partial(expert_kernel, half, size, steps), grid=...]
    gather x20 -> x0, local copies, waits for them, and re-layouts: 13.3 us -> none  [the longest x4 7.44 us: finish(): picked = jnp.take(summed, flat_slot, axis=0)]
    dot_general x6 -> x0, matrix products: 11.8 us -> none  [the longest x1 7.89 us: expert_apply(): jnp.dot(hidden, down_weight, preferred_element_type=jnp.float32)]
    unnamed x9 -> x21, local copies, waits for them, and re-layouts: 0.81 us -> 11.2 us
    ppermute x3 -> x22, waiting for transfers between devices: 21.3 us -> 27.3 us  [moved(): return lax.ppermute(block, HOME, pairs)]
  transfers between devices with their start and end apart: 4 -> 22, of which waited for: 4 -> 5; matrix products, arithmetic and copies ran while one was open for 4% -> 1% of each run, Pallas kernels for 0% -> 11%
where the time goes in v1:
time: 104 us; the launch traced here: 103 us
  starting transfers between devices  49.6 us (48%)
  waiting for transfers between devices  27.3 us (26%)
  Pallas kernels  14 us (13%)
  local copies, waits for them, and re-layouts  11.6 us (11%)
    ppermute x22, starting transfers between devices, moved(): return lax.ppermute(block, HOME, pairs)  49.6 us
    ppermute x22, waiting for transfers between devices, moved(): return lax.ppermute(block, HOME, pairs)  27.3 us
    unnamed x21, local copies, waits for them, and re-layouts  11.2 us
    pallas_call x2, Pallas kernels, run_experts(): pl.pallas_call(functools.partial(expert_kernel, half, size, steps), grid=...  10.4 us
    pallas_call x1, Pallas kernels, shards(): pl.pallas_call(functools.partial(combine_kernel, [size for _, size in par...  2.35 us
  transfers between devices with their start and end apart: 22, of which 5 were waited for; matrix products, arithmetic and copies ran while one was open for 1% of the time, Pallas kernels for 11%

profile of v1, /device:TPU:0, one launch (start us, length us, event | category | flops | bytes accessed | tf_op | source)
XLA Modules:
  0.0 103.1 jit_solution(2525334403974111664)
XLA Ops:
  0.0 0.7 copy.8
  0.8 1.0 %copy-done.6 = bf16[1,2,64,2048]{3,2,1,0:T(8,128)(2,1)S(1)} copy-done((bf16[1,2,64,2048]{3,2,1,0:T(8,128)(2,1)S(1)}, bf16[1,2,64,2048]{3,2,1,0:T(8,128)(2,1)}, u32[]{:S(2)}) %copy-start.6) | copy-done | bytes 524312
  1.8 0.8 pack.1
  2.6 3.0 %collective-permute-start.2 = (bf16[32,2048]{1,0:T(8,128)(2,1)S(1)}, bf16[32,2048]{1,0:T(8,128)(2,1)S(1)}, u32[]{:S(2)}, u32[]{:S(2)}) collective-permute-start(bf16[32,2048]{1,0:T(8,128)(2,1)S(1)} %get-tuple-element.21), channel_id=1, source_target_pairs={{0,8},{1,9},{2,10},{3,11},{4,12},{5,13},{6,14},{7,15},{8,16},{9,17... | collective-permute-start | bytes 393224 | tf_op jit(solution)/shard_map/ppermute | solution.py:23
  5.6 2.5 %collective-permute-start.3 = (bf16[32,2048]{1,0:T(8,128)(2,1)S(1)}, bf16[32,2048]{1,0:T(8,128)(2,1)S(1)}, u32[]{:S(2)}, u32[]{:S(2)}) collective-permute-start(bf16[32,2048]{1,0:T(8,128)(2,1)S(1)} %get-tuple-element.22), channel_id=1, source_target_pairs={{0,10},{1,11},{2,8},{3,9},{4,14},{5,15},{6,12},{7,13},{8,18},{9,19... | collective-permute-start | bytes 393224 | tf_op jit(solution)/shard_map/ppermute | solution.py:23
  8.1 3.5 %collective-permute-start.4 = (bf16[32,2048]{1,0:T(8,128)(2,1)S(1)}, bf16[32,2048]{1,0:T(8,128)(2,1)S(1)}, u32[]{:S(2)}, u32[]{:S(2)}) collective-permute-start(bf16[32,2048]{1,0:T(8,128)(2,1)S(1)} %get-tuple-element.23), channel_id=1, source_target_pairs={{0,12},{1,13},{2,14},{3,15},{4,8},{5,9},{6,10},{7,11},{8,20},{9,21... | collective-permute-start | bytes 393224 | tf_op jit(solution)/shard_map/ppermute | solution.py:23
  11.6 1.6 %collective-permute-start.12 = (bf16[48,2048]{1,0:T(8,128)(2,1)S(1)}, bf16[48,2048]{1,0:T(8,128)(2,1)S(1)}, u32[]{:S(2)}, u32[]{:S(2)}) collective-permute-start(bf16[48,2048]{1,0:T(8,128)(2,1)S(1)} %get-tuple-element.27), channel_id=1, source_target_pairs={{0,8},{1,9},{2,10},{3,11},{4,12},{5,13},{6,14},{7,15},{8,16},{9,17... | collective-permute-start | bytes 589832 | tf_op jit(solution)/shard_map/ppermute | solution.py:23
  13.3 0.1 collective-permute-done.2.refs_0_
  13.4 3.2 %collective-permute-start.13 = (bf16[48,2048]{1,0:T(8,128)(2,1)S(1)}, bf16[48,2048]{1,0:T(8,128)(2,1)S(1)}, u32[]{:S(2)}, u32[]{:S(2)}) collective-permute-start(bf16[48,2048]{1,0:T(8,128)(2,1)S(1)} %get-tuple-element.28), channel_id=1, source_target_pairs={{0,10},{1,11},{2,8},{3,9},{4,14},{5,15},{6,12},{7,13},{8,18},{9,19... | collective-permute-start | bytes 589832 | tf_op jit(solution)/shard_map/ppermute | solution.py:23
  16.7 10.6 %collective-permute-start.14 = (bf16[48,2048]{1,0:T(8,128)(2,1)S(1)}, bf16[48,2048]{1,0:T(8,128)(2,1)S(1)}, u32[]{:S(2)}, u32[]{:S(2)}) collective-permute-start(bf16[48,2048]{1,0:T(8,128)(2,1)S(1)} %get-tuple-element.29), channel_id=1, source_target_pairs={{0,12},{1,13},{2,14},{3,15},{4,8},{5,9},{6,10},{7,11},{8,20},{9,21... | collective-permute-start | bytes 589832 | tf_op jit(solution)/shard_map/ppermute | solution.py:23
  27.4 3.6 %collective-permute-done.12.refs_0_ = bf16[48,2048]{1,0:T(8,128)(2,1)S(1)} collective-permute-done((bf16[48,2048]{1,0:T(8,128)(2,1)S(1)}, bf16[48,2048]{1,0:T(8,128)(2,1)S(1)}, u32[]{:S(2)}, u32[]{:S(2)}) %collective-permute-start.12) | collective-permute-done | bytes 196640 | tf_op jit(solution)/shard_map/ppermute | solution.py:23
  31.0 2.3 %collective-permute-start.1 = (bf16[8,2048]{1,0:T(8,128)(2,1)}, bf16[8,2048]{1,0:T(8,128)(2,1)S(1)}, u32[]{:S(2)}, u32[]{:S(2)}) collective-permute-start(bf16[8,2048]{1,0:T(8,128)(2,1)} %bitcast.27), channel_id=1, source_target_pairs={{0,24},{1,25},{2,26},{3,27},{4,28},{5,29},{6,30},{7,31},{8,0},{9,1... | collective-permute-start | bytes 98312 | tf_op jit(solution)/shard_map/ppermute | solution.py:23
  33.4 4.6 %collective-permute-done.14.refs_2_ = bf16[48,2048]{1,0:T(8,128)(2,1)S(1)} collective-permute-done((bf16[48,2048]{1,0:T(8,128)(2,1)S(1)}, bf16[48,2048]{1,0:T(8,128)(2,1)S(1)}, u32[]{:S(2)}, u32[]{:S(2)}) %collective-permute-start.14) | collective-permute-done | bytes 196640 | tf_op jit(solution)/shard_map/ppermute | solution.py:23
  38.2 2.2 %copy-done = bf16[1,2048,1024]{2,1,0:T(8,128)(2,1)S(1)} copy-done((bf16[1,2048,1024]{2,1,0:T(8,128)(2,1)S(1)}, bf16[1,2048,1024]{2,1,0:T(8,128)(2,1)}, u32[]{:S(2)}) %copy-start) | copy-done | bytes 4194328
  40.4 2.2 %copy-done.2 = bf16[1,2048,1024]{2,1,0:T(8,128)(2,1)S(1)} copy-done((bf16[1,2048,1024]{2,1,0:T(8,128)(2,1)S(1)}, bf16[1,2048,1024]{2,1,0:T(8,128)(2,1)}, u32[]{:S(2)}) %copy-start.2) | copy-done | bytes 4194328
  42.6 2.2 %copy-done.4 = bf16[1,1024,2048]{2,1,0:T(8,128)(2,1)S(1)} copy-done((bf16[1,1024,2048]{2,1,0:T(8,128)(2,1)S(1)}, bf16[1,1024,2048]{2,1,0:T(8,128)(2,1)}, u32[]{:S(2)}) %copy-start.4) | copy-done | bytes 4194328
  44.8 0.7 copy-done.8
  45.5 4.7 %experts.2 = (bf16[64,2048]{1,0:T(8,128)(2,1)S(1)}, bf16[64,2048]{1,0:T(8,128)(2,1)S(1)}) custom-call(bf16[32,2048]{1,0:T(8,128)(2,1)S(1)} %collective-permute-done.2.refs_0_, bf16[32,2048]{1,0:T(8,128)(2,1)S(1)} %collective-permute-done.3.refs_1_, bf16[32,2048]{1,0:T(8,128)(2,1)S(1)} %collective-permute-done.4.refs_2_, ...), custom_call_target="tpu_custom_call" | custom-call | flops 1610612736 | bytes 14680064 | tf_op jit(solution)/shard_map/experts/pallas_call | solution.py:143
  50.2 0.6 collective-permute-start.7
  50.8 2.2 %copy-done.5 = bf16[1,1024,2048]{2,1,0:T(8,128)(2,1)S(1)} copy-done((bf16[1,1024,2048]{2,1,0:T(8,128)(2,1)S(1)}, bf16[1,1024,2048]{2,1,0:T(8,128)(2,1)}, u32[]{:S(2)}) %copy-start.5) | copy-done | bytes 4194328
  53.0 5.7 %experts.3 = (bf16[96,2048]{1,0:T(8,128)(2,1)S(1)}, bf16[96,2048]{1,0:T(8,128)(2,1)S(1)}) custom-call(bf16[48,2048]{1,0:T(8,128)(2,1)S(1)} %collective-permute-done.12.refs_0_, bf16[48,2048]{1,0:T(8,128)(2,1)S(1)} %collective-permute-done.13.refs_1_, bf16[48,2048]{1,0:T(8,128)(2,1)S(1)} %collective-permute-done.14.refs_2_, ...), custom_call_target="tpu_custom_call" | custom-call | flops 2415919104 | bytes 15728640 | tf_op jit(solution)/shard_map/experts/pallas_call | solution.py:143
  58.9 3.8 %collective-permute-start.11 = (bf16[32,2048]{1,0:T(8,128)(2,1)S(1)}, bf16[32,2048]{1,0:T(8,128)(2,1)S(1)}, u32[]{:S(2)}, u32[]{:S(2)}) collective-permute-start(bf16[32,2048]{1,0:T(8,128)(2,1)S(1)} %pad_maximum_fusion.9), channel_id=1, source_target_pairs={{0,30},{1,31},{2,28},{3,29},{4,26},{5,27},{6,24},{7,25},{8,6},{9,7... | collective-permute-start | bytes 393224 | tf_op jit(solution)/shard_map/ppermute | solution.py:23
  62.7 2.5 %collective-permute-start.10 = (bf16[32,2048]{1,0:T(8,128)(2,1)S(1)}, bf16[32,2048]{1,0:T(8,128)(2,1)S(1)}, u32[]{:S(2)}, u32[]{:S(2)}) collective-permute-start(bf16[32,2048]{1,0:T(8,128)(2,1)S(1)} %pad_maximum_fusion.8), channel_id=1, source_target_pairs={{0,28},{1,29},{2,30},{3,31},{4,24},{5,25},{6,26},{7,27},{8,4},{9,5... | collective-permute-start | bytes 393224 | tf_op jit(solution)/shard_map/ppermute | solution.py:23
  65.2 1.4 %collective-permute-start.9 = (bf16[32,2048]{1,0:T(8,128)(2,1)S(1)}, bf16[32,2048]{1,0:T(8,128)(2,1)S(1)}, u32[]{:S(2)}, u32[]{:S(2)}) collective-permute-start(bf16[32,2048]{1,0:T(8,128)(2,1)S(1)} %pad_maximum_fusion.7), channel_id=1, source_target_pairs={{0,26},{1,27},{2,24},{3,25},{4,30},{5,31},{6,28},{7,29},{8,2},{9,3... | collective-permute-start | bytes 393224 | tf_op jit(solution)/shard_map/ppermute | solution.py:23
  66.8 3.8 %collective-permute-start.21 = (bf16[48,2048]{1,0:T(8,128)(2,1)S(1)}, bf16[48,2048]{1,0:T(8,128)(2,1)S(1)}, u32[]{:S(2)}, u32[]{:S(2)}) collective-permute-start(bf16[48,2048]{1,0:T(8,128)(2,1)S(1)} %pad_maximum_fusion.5), channel_id=1, source_target_pairs={{0,30},{1,31},{2,28},{3,29},{4,26},{5,27},{6,24},{7,25},{8,6},{9,7... | collective-permute-start | bytes 589832 | tf_op jit(solution)/shard_map/ppermute | solution.py:23
  70.6 6.9 %collective-permute-start.19 = (bf16[48,2048]{1,0:T(8,128)(2,1)S(1)}, bf16[48,2048]{1,0:T(8,128)(2,1)S(1)}, u32[]{:S(2)}, u32[]{:S(2)}) collective-permute-start(bf16[48,2048]{1,0:T(8,128)(2,1)S(1)} %pad_maximum_fusion.3), channel_id=1, source_target_pairs={{0,26},{1,27},{2,24},{3,25},{4,30},{5,31},{6,28},{7,29},{8,2},{9,3... | collective-permute-start | bytes 589832 | tf_op jit(solution)/shard_map/ppermute | solution.py:23
  77.5 6.9 %collective-permute-done.10.refs_4_ = bf16[32,2048]{1,0:T(8,128)(2,1)S(1)} collective-permute-done((bf16[32,2048]{1,0:T(8,128)(2,1)S(1)}, bf16[32,2048]{1,0:T(8,128)(2,1)S(1)}, u32[]{:S(2)}, u32[]{:S(2)}) %collective-permute-start.10) | collective-permute-done | bytes 131104 | tf_op jit(solution)/shard_map/ppermute | solution.py:23
  84.5 3.4 %collective-permute-start.18 = (bf16[48,2048]{1,0:T(8,128)(2,1)S(1)}, bf16[48,2048]{1,0:T(8,128)(2,1)S(1)}, u32[]{:S(2)}, u32[]{:S(2)}) collective-permute-start(bf16[48,2048]{1,0:T(8,128)(2,1)S(1)} %pad_maximum_fusion.2), channel_id=1, source_target_pairs={{0,24},{1,25},{2,26},{3,27},{4,28},{5,29},{6,30},{7,31},{8,0},{9,1... | collective-permute-start | bytes 589832 | tf_op jit(solution)/shard_map/ppermute | solution.py:23
  88.0 0.5 weights.1
  88.6 0.1 copy.9
  88.7 12.0 %collective-permute-done.8.refs_2_ = bf16[32,2048]{1,0:T(8,128)(2,1)S(1)} collective-permute-done((bf16[32,2048]{1,0:T(8,128)(2,1)S(1)}, bf16[32,2048]{1,0:T(8,128)(2,1)S(1)}, u32[]{:S(2)}, u32[]{:S(2)}) %collective-permute-start.8) | collective-permute-done | bytes 131104 | tf_op jit(solution)/shard_map/ppermute | solution.py:23
  100.7 2.4 %combine.1 = bf16[128,2048]{1,0:T(8,128)(2,1)} custom-call(bf16[128,2048]{1,0:T(8,128)(2,1)S(1)} %bitcast.22, bf16[2,128,128]{2,1,0:T(8,128)(2,1)S(1)} %bitcast.24, bf16[2,128,192]{2,1,0:T(8,128)(2,1)S(1)} %bitcast.23, bf16[32,2048]{1,0:T(8,128)(2,1)S(1)} %collective-permute-done.8.refs_2_, bf16[32,2048]{1,0:T(8,128)(2,1)S(1)} %collective-permute-done.9.refs_3_, ...), custom_call_target="tpu_custom_call" | custom-call | tf_op jit(solution)/shard_map/combine/pallas_call | solution.py:230
  (63 shorter events, 1.0 us)
Async XLA Ops:
  0.8 1.0 %copy-start.6 = (bf16[1,2,64,2048]{3,2,1,0:T(8,128)(2,1)S(1)}, bf16[1,2,64,2048]{3,2,1,0:T(8,128)(2,1)}, u32[]{:S(2)}) copy-start(bf16[1,2,64,2048]{3,2,1,0:T(8,128)(2,1)} %param.7) | copy-start | bytes 1572868
  2.6 10.8 %collective-permute-start.2 = (bf16[32,2048]{1,0:T(8,128)(2,1)S(1)}, bf16[32,2048]{1,0:T(8,128)(2,1)S(1)}, u32[]{:S(2)}, u32[]{:S(2)}) collective-permute-start(bf16[32,2048]{1,0:T(8,128)(2,1)S(1)} %get-tuple-element.21), channel_id=1, source_target_pairs={{0,8},{1,9},{2,10},{3,11},{4,12},{5,13},{6,14},{7,15},{8,16},{9,17... | collective-permute-start | bytes 393224 | tf_op jit(solution)/shard_map/ppermute | solution.py:23
  5.6 11.0 %collective-permute-start.3 = (bf16[32,2048]{1,0:T(8,128)(2,1)S(1)}, bf16[32,2048]{1,0:T(8,128)(2,1)S(1)}, u32[]{:S(2)}, u32[]{:S(2)}) collective-permute-start(bf16[32,2048]{1,0:T(8,128)(2,1)S(1)} %get-tuple-element.22), channel_id=1, source_target_pairs={{0,10},{1,11},{2,8},{3,9},{4,14},{5,15},{6,12},{7,13},{8,18},{9,19... | collective-permute-start | bytes 393224 | tf_op jit(solution)/shard_map/ppermute | solution.py:23
  8.1 19.1 %collective-permute-start.4 = (bf16[32,2048]{1,0:T(8,128)(2,1)S(1)}, bf16[32,2048]{1,0:T(8,128)(2,1)S(1)}, u32[]{:S(2)}, u32[]{:S(2)}) collective-permute-start(bf16[32,2048]{1,0:T(8,128)(2,1)S(1)} %get-tuple-element.23), channel_id=1, source_target_pairs={{0,12},{1,13},{2,14},{3,15},{4,8},{5,9},{6,10},{7,11},{8,20},{9,21... | collective-permute-start | bytes 393224 | tf_op jit(solution)/shard_map/ppermute | solution.py:23
  11.6 15.7 %collective-permute-start.5 = (bf16[32,2048]{1,0:T(8,128)(2,1)S(1)}, bf16[32,2048]{1,0:T(8,128)(2,1)S(1)}, u32[]{:S(2)}, u32[]{:S(2)}) collective-permute-start(bf16[32,2048]{1,0:T(8,128)(2,1)S(1)} %get-tuple-element.24), channel_id=1, source_target_pairs={{0,14},{1,15},{2,12},{3,13},{4,10},{5,11},{6,8},{7,9},{8,22},{9,23... | collective-permute-start | bytes 393224 | tf_op jit(solution)/shard_map/ppermute | solution.py:23
  11.6 19.4 %collective-permute-start.12 = (bf16[48,2048]{1,0:T(8,128)(2,1)S(1)}, bf16[48,2048]{1,0:T(8,128)(2,1)S(1)}, u32[]{:S(2)}, u32[]{:S(2)}) collective-permute-start(bf16[48,2048]{1,0:T(8,128)(2,1)S(1)} %get-tuple-element.27), channel_id=1, source_target_pairs={{0,8},{1,9},{2,10},{3,11},{4,12},{5,13},{6,14},{7,15},{8,16},{9,17... | collective-permute-start | bytes 589832 | tf_op jit(solution)/shard_map/ppermute | solution.py:23
  13.4 19.9 %collective-permute-start.13 = (bf16[48,2048]{1,0:T(8,128)(2,1)S(1)}, bf16[48,2048]{1,0:T(8,128)(2,1)S(1)}, u32[]{:S(2)}, u32[]{:S(2)}) collective-permute-start(bf16[48,2048]{1,0:T(8,128)(2,1)S(1)} %get-tuple-element.28), channel_id=1, source_target_pairs={{0,10},{1,11},{2,8},{3,9},{4,14},{5,15},{6,12},{7,13},{8,18},{9,19... | collective-permute-start | bytes 589832 | tf_op jit(solution)/shard_map/ppermute | solution.py:23
  16.7 21.4 %collective-permute-start.14 = (bf16[48,2048]{1,0:T(8,128)(2,1)S(1)}, bf16[48,2048]{1,0:T(8,128)(2,1)S(1)}, u32[]{:S(2)}, u32[]{:S(2)}) collective-permute-start(bf16[48,2048]{1,0:T(8,128)(2,1)S(1)} %get-tuple-element.29), channel_id=1, source_target_pairs={{0,12},{1,13},{2,14},{3,15},{4,8},{5,9},{6,10},{7,11},{8,20},{9,21... | collective-permute-start | bytes 589832 | tf_op jit(solution)/shard_map/ppermute | solution.py:23
  27.2 10.8 %collective-permute-start.15 = (bf16[48,2048]{1,0:T(8,128)(2,1)S(1)}, bf16[48,2048]{1,0:T(8,128)(2,1)S(1)}, u32[]{:S(2)}, u32[]{:S(2)}) collective-permute-start(bf16[48,2048]{1,0:T(8,128)(2,1)S(1)} %get-tuple-element.30), channel_id=1, source_target_pairs={{0,14},{1,15},{2,12},{3,13},{4,10},{5,11},{6,8},{7,9},{8,22},{9,23... | collective-permute-start | bytes 589832 | tf_op jit(solution)/shard_map/ppermute | solution.py:23
  27.4 10.8 %collective-permute-start.6 = (bf16[64,2048]{1,0:T(8,128)(2,1)S(1)}, bf16[64,2048]{1,0:T(8,128)(2,1)S(1)}, u32[]{:S(2)}, u32[]{:S(2)}) collective-permute-start(bf16[64,2048]{1,0:T(8,128)(2,1)S(1)} %pad_maximum_fusion.1), channel_id=1, source_target_pairs={{0,1},{1,0},{2,3},{3,2},{4,5},{5,4},{6,7},{7,6},{8,9},{9,8},{10,11... | collective-permute-start | bytes 786440 | tf_op jit(solution)/shard_map/ppermute | solution.py:23
  31.0 39.6 %collective-permute-start.1 = (bf16[8,2048]{1,0:T(8,128)(2,1)}, bf16[8,2048]{1,0:T(8,128)(2,1)S(1)}, u32[]{:S(2)}, u32[]{:S(2)}) collective-permute-start(bf16[8,2048]{1,0:T(8,128)(2,1)} %bitcast.27), channel_id=1, source_target_pairs={{0,24},{1,25},{2,26},{3,27},{4,28},{5,29},{6,30},{7,31},{8,0},{9,1... | collective-permute-start | bytes 98312 | tf_op jit(solution)/shard_map/ppermute | solution.py:23
  33.3 33.4 %collective-permute-start = (bf16[1,2048]{1,0:T(2,128)(2,1)}, bf16[1,2048]{1,0:T(2,128)(2,1)S(1)}, u32[]{:S(2)}, u32[]{:S(2)}) collective-permute-start(bf16[1,2048]{1,0:T(2,128)(2,1)} %refs_5_.3), channel_id=1, source_target_pairs={{0,24},{1,25},{2,26},{3,27},{4,28},{5,29},{6,30},{7,31},{8,0},{9,1... | collective-permute-start | bytes 12296 | tf_op jit(solution)/shard_map/ppermute | solution.py:23
  38.1 12.6 %collective-permute-start.16 = (bf16[96,2048]{1,0:T(8,128)(2,1)S(1)}, bf16[96,2048]{1,0:T(8,128)(2,1)S(1)}, u32[]{:S(2)}, u32[]{:S(2)}) collective-permute-start(bf16[96,2048]{1,0:T(8,128)(2,1)S(1)} %pad_maximum_fusion), channel_id=1, source_target_pairs={{0,1},{1,0},{2,3},{3,2},{4,5},{5,4},{6,7},{7,6},{8,9},{9,8},{10,11... | collective-permute-start | bytes 1179656 | tf_op jit(solution)/shard_map/ppermute | solution.py:23
  38.2 2.2 %copy-start = (bf16[1,2048,1024]{2,1,0:T(8,128)(2,1)S(1)}, bf16[1,2048,1024]{2,1,0:T(8,128)(2,1)}, u32[]{:S(2)}) copy-start(bf16[1,2048,1024]{2,1,0:T(8,128)(2,1)} %param.11) | copy-start | bytes 12582916
  40.4 2.2 %copy-start.2 = (bf16[1,2048,1024]{2,1,0:T(8,128)(2,1)S(1)}, bf16[1,2048,1024]{2,1,0:T(8,128)(2,1)}, u32[]{:S(2)}) copy-start(bf16[1,2048,1024]{2,1,0:T(8,128)(2,1)} %param.12) | copy-start | bytes 12582916
  42.6 2.2 %copy-start.4 = (bf16[1,1024,2048]{2,1,0:T(8,128)(2,1)S(1)}, bf16[1,1024,2048]{2,1,0:T(8,128)(2,1)}, u32[]{:S(2)}) copy-start(bf16[1,1024,2048]{2,1,0:T(8,128)(2,1)} %param.13) | copy-start | bytes 12582916
  44.8 0.7 copy-start.8
  45.5 5.3 %copy-start.1 = (bf16[1,2048,1024]{2,1,0:T(8,128)(2,1)S(1)}, bf16[1,2048,1024]{2,1,0:T(8,128)(2,1)}, u32[]{:S(2)}) copy-start(bf16[1,2048,1024]{2,1,0:T(8,128)(2,1)} %param.11) | copy-start | bytes 12582916
  45.5 5.3 %copy-start.3 = (bf16[1,2048,1024]{2,1,0:T(8,128)(2,1)S(1)}, bf16[1,2048,1024]{2,1,0:T(8,128)(2,1)}, u32[]{:S(2)}) copy-start(bf16[1,2048,1024]{2,1,0:T(8,128)(2,1)} %param.12) | copy-start | bytes 12582916
  45.5 5.3 %copy-start.9 = (bf16[1,2048]{1,0:T(2,128)(2,1)S(1)}, bf16[1,2048]{1,0:T(2,128)(2,1)}, u32[]{:S(2)}) copy-start(bf16[1,2048]{1,0:T(2,128)(2,1)} %refs_5_.3) | copy-start | bytes 12292
  50.2 8.7 %collective-permute-start.7 = (bf16[64,2048]{1,0:T(8,128)(2,1)S(1)}, bf16[64,2048]{1,0:T(8,128)(2,1)S(1)}, u32[]{:S(2)}, u32[]{:S(2)}) collective-permute-start(bf16[64,2048]{1,0:T(8,128)(2,1)S(1)} %get-tuple-element.26), channel_id=1, source_target_pairs={{0,1},{1,0},{2,3},{3,2},{4,5},{5,4},{6,7},{7,6},{8,9},{9,8},{10,11... | collective-permute-start | bytes 786440 | tf_op jit(solution)/shard_map/ppermute | solution.py:23
  50.8 2.2 %copy-start.5 = (bf16[1,1024,2048]{2,1,0:T(8,128)(2,1)S(1)}, bf16[1,1024,2048]{2,1,0:T(8,128)(2,1)}, u32[]{:S(2)}) copy-start(bf16[1,1024,2048]{2,1,0:T(8,128)(2,1)} %param.13) | copy-start | bytes 12582916
  58.7 29.3 %copy-start.7 = (bf16[1,2,64,2048]{3,2,1,0:T(8,128)(2,1)S(1)}, bf16[1,2,64,2048]{3,2,1,0:T(8,128)(2,1)}, u32[]{:S(2)}) copy-start(bf16[1,2,64,2048]{3,2,1,0:T(8,128)(2,1)} %param.7) | copy-start | bytes 1572868
  58.7 6.5 %collective-permute-start.17 = (bf16[96,2048]{1,0:T(8,128)(2,1)S(1)}, bf16[96,2048]{1,0:T(8,128)(2,1)S(1)}, u32[]{:S(2)}, u32[]{:S(2)}) collective-permute-start(bf16[96,2048]{1,0:T(8,128)(2,1)S(1)} %get-tuple-element.32), channel_id=1, source_target_pairs={{0,1},{1,0},{2,3},{3,2},{4,5},{5,4},{6,7},{7,6},{8,9},{9,8},{10,11... | collective-permute-start | bytes 1179656 | tf_op jit(solution)/shard_map/ppermute | solution.py:23
  58.9 11.7 %collective-permute-start.11 = (bf16[32,2048]{1,0:T(8,128)(2,1)S(1)}, bf16[32,2048]{1,0:T(8,128)(2,1)S(1)}, u32[]{:S(2)}, u32[]{:S(2)}) collective-permute-start(bf16[32,2048]{1,0:T(8,128)(2,1)S(1)} %pad_maximum_fusion.9), channel_id=1, source_target_pairs={{0,30},{1,31},{2,28},{3,29},{4,26},{5,27},{6,24},{7,25},{8,6},{9,7... | collective-permute-start | bytes 393224 | tf_op jit(solution)/shard_map/ppermute | solution.py:23
  62.7 21.8 %collective-permute-start.10 = (bf16[32,2048]{1,0:T(8,128)(2,1)S(1)}, bf16[32,2048]{1,0:T(8,128)(2,1)S(1)}, u32[]{:S(2)}, u32[]{:S(2)}) collective-permute-start(bf16[32,2048]{1,0:T(8,128)(2,1)S(1)} %pad_maximum_fusion.8), channel_id=1, source_target_pairs={{0,28},{1,29},{2,30},{3,31},{4,24},{5,25},{6,26},{7,27},{8,4},{9,5... | collective-permute-start | bytes 393224 | tf_op jit(solution)/shard_map/ppermute | solution.py:23
  65.2 22.7 %collective-permute-start.9 = (bf16[32,2048]{1,0:T(8,128)(2,1)S(1)}, bf16[32,2048]{1,0:T(8,128)(2,1)S(1)}, u32[]{:S(2)}, u32[]{:S(2)}) collective-permute-start(bf16[32,2048]{1,0:T(8,128)(2,1)S(1)} %pad_maximum_fusion.7), channel_id=1, source_target_pairs={{0,26},{1,27},{2,24},{3,25},{4,30},{5,31},{6,28},{7,29},{8,2},{9,3... | collective-permute-start | bytes 393224 | tf_op jit(solution)/shard_map/ppermute | solution.py:23
  66.8 33.9 %collective-permute-start.21 = (bf16[48,2048]{1,0:T(8,128)(2,1)S(1)}, bf16[48,2048]{1,0:T(8,128)(2,1)S(1)}, u32[]{:S(2)}, u32[]{:S(2)}) collective-permute-start(bf16[48,2048]{1,0:T(8,128)(2,1)S(1)} %pad_maximum_fusion.5), channel_id=1, source_target_pairs={{0,30},{1,31},{2,28},{3,29},{4,26},{5,27},{6,24},{7,25},{8,6},{9,7... | collective-permute-start | bytes 589832 | tf_op jit(solution)/shard_map/ppermute | solution.py:23
  70.6 30.1 %collective-permute-start.20 = (bf16[48,2048]{1,0:T(8,128)(2,1)S(1)}, bf16[48,2048]{1,0:T(8,128)(2,1)S(1)}, u32[]{:S(2)}, u32[]{:S(2)}) collective-permute-start(bf16[48,2048]{1,0:T(8,128)(2,1)S(1)} %pad_maximum_fusion.4), channel_id=1, source_target_pairs={{0,28},{1,29},{2,30},{3,31},{4,24},{5,25},{6,26},{7,27},{8,4},{9,5... | collective-permute-start | bytes 589832 | tf_op jit(solution)/shard_map/ppermute | solution.py:23
  70.6 30.1 %collective-permute-start.19 = (bf16[48,2048]{1,0:T(8,128)(2,1)S(1)}, bf16[48,2048]{1,0:T(8,128)(2,1)S(1)}, u32[]{:S(2)}, u32[]{:S(2)}) collective-permute-start(bf16[48,2048]{1,0:T(8,128)(2,1)S(1)} %pad_maximum_fusion.3), channel_id=1, source_target_pairs={{0,26},{1,27},{2,24},{3,25},{4,30},{5,31},{6,28},{7,29},{8,2},{9,3... | collective-permute-start | bytes 589832 | tf_op jit(solution)/shard_map/ppermute | solution.py:23
  84.5 16.2 %collective-permute-start.18 = (bf16[48,2048]{1,0:T(8,128)(2,1)S(1)}, bf16[48,2048]{1,0:T(8,128)(2,1)S(1)}, u32[]{:S(2)}, u32[]{:S(2)}) collective-permute-start(bf16[48,2048]{1,0:T(8,128)(2,1)S(1)} %pad_maximum_fusion.2), channel_id=1, source_target_pairs={{0,24},{1,25},{2,26},{3,27},{4,28},{5,29},{6,30},{7,31},{8,0},{9,1... | collective-permute-start | bytes 589832 | tf_op jit(solution)/shard_map/ppermute | solution.py:23
  87.9 12.8 %collective-permute-start.8 = (bf16[32,2048]{1,0:T(8,128)(2,1)S(1)}, bf16[32,2048]{1,0:T(8,128)(2,1)S(1)}, u32[]{:S(2)}, u32[]{:S(2)}) collective-permute-start(bf16[32,2048]{1,0:T(8,128)(2,1)S(1)} %pad_maximum_fusion.6), channel_id=1, source_target_pairs={{0,24},{1,25},{2,26},{3,27},{4,28},{5,29},{6,30},{7,31},{8,0},{9,1... | collective-permute-start | bytes 393224 | tf_op jit(solution)/shard_map/ppermute | solution.py:23

commit v2 on v1

v2 whole, which is shorter than its diff:
```python
import functools

import jax
import jax.numpy as jnp
from jax import lax
from jax.experimental import pallas as pl
from jax.experimental.pallas import tpu as pltpu
from jax.sharding import PartitionSpec as P

CAP = 20
epsilon = 1e-06
HOME = ("section", "expert")


def moved(block, by, flip):
    sections, width = lax.axis_size("section"), lax.axis_size("expert")
    pairs = [
        (s * width + e, (s + by) % sections * width + (e ^ flip))
        for s in range(sections)
        for e in range(width)
    ]
    return lax.ppermute(block, HOME, pairs)


def ranks(me, chosen, width, groups):
    tokens = chosen.shape[1]
    owner = lax.broadcasted_iota(jnp.int32, (width, tokens), 0) ^ me
    expert = owner // groups if groups > 1 else owner
    first = chosen[0:1, :] == expert
    match = first | (chosen[1:2, :] == expert)
    before = lax.broadcasted_iota(jnp.int32, (tokens, tokens), 0) < lax.broadcasted_iota(
        jnp.int32, (tokens, tokens), 1
    )
    rank = jnp.dot(
        match.astype(jnp.bfloat16), before.astype(jnp.bfloat16), preferred_element_type=jnp.float32
    ).astype(jnp.int32)
    return first, jnp.where(match, rank, -1)


def side_by_side(chosen_ref):
    return jnp.concatenate([chosen_ref[b] for b in range(chosen_ref.shape[0])], axis=1)


def pack_kernel(width, groups, flips, size, me_ref, *refs):
    chosen_refs, rows_refs, out_refs = refs[0:2], refs[2:4], refs[4:]
    for part in range(2):
        _, rank = ranks(me_ref[0], side_by_side(chosen_refs[part]), width, groups)
        rows = rows_refs[part][...]
        place = lax.broadcasted_iota(jnp.int32, (size, rank.shape[1]), 0)
        for out_ref, i in zip(out_refs, flips):
            select = (rank[i : i + 1] == place).astype(jnp.bfloat16)
            out_ref[part * size : (part + 1) * size] = jnp.dot(
                select, rows, preferred_element_type=jnp.float32
            ).astype(jnp.bfloat16)


def weight_kernel(
    width, groups, teams, size, me_ref, chosen_ref, rows_ref, there_ref, *out_refs
):
    chosen = side_by_side(chosen_ref)
    first, rank = ranks(me_ref[0], chosen, width, groups)
    experts = width // groups
    normed = normalised(rows_ref[...], there_ref[experts : experts + 1])
    logits = lax.dot_general(
        there_ref[0:experts], normed, (((1,), (1,)), ((), ())), preferred_element_type=jnp.float32
    )
    names = lax.broadcasted_iota(jnp.int32, logits.shape, 0)
    one = jnp.sum(jnp.where(names == chosen[0:1, :], logits, 0.0), axis=0, keepdims=True)
    two = jnp.sum(jnp.where(names == chosen[1:2, :], logits, 0.0), axis=0, keepdims=True)
    top = jnp.maximum(one, two)
    one, two = jnp.exp(one - top), jnp.exp(two - top)
    total = one + two
    weight = jnp.where(first, one / total, two / total)
    place = lax.broadcasted_iota(jnp.int32, (size, rank.shape[1]), 0)
    for part, team in enumerate(teams):
        for at, i in enumerate(team + tuple(i + 1 for i in team)):
            wide = jnp.where(rank[i : i + 1] == place, weight[i : i + 1], 0.0)
            high = wide.astype(jnp.bfloat16)
            span = slice(at * size, (at + 1) * size)
            out_refs[part][span] = high
            out_refs[2 + part][span] = (wide - high.astype(jnp.float32)).astype(jnp.bfloat16)


def normalised(rows, gain):
    wide = rows.astype(jnp.float32)
    scale = lax.rsqrt(jnp.mean(wide * wide, axis=-1, keepdims=True) + epsilon)
    return (wide * scale * gain.astype(jnp.float32)).astype(jnp.bfloat16)


def load_kernel(*refs):
    count = len(refs) // 2
    sources, held, sems = refs[:count], refs[count:-1], refs[-1]
    copies = [
        pltpu.make_async_copy(source, place, sems.at[k])
        for k, (source, place) in enumerate(zip(sources, held))
    ]
    for copy in copies:
        copy.start()
    for copy in copies:
        copy.wait()


def expert_kernel(count, size, *refs):
    blocks, (gain_ref, gate_ref, up_ref, down_ref) = refs[:count], refs[count : count + 4]
    outs, (normed_ref, hidden_ref) = refs[-2 - count : -2], refs[-2:]
    gain = gain_ref[...]
    for j in range(count):
        normed_ref[j * size : (j + 1) * size] = normalised(blocks[j][0:size], gain)
    normed = normed_ref[...]
    units, features = down_ref.shape
    step = min(256, units)
    for at in range(0, units, step):
        span = slice(at, at + step)
        gate = jnp.dot(normed, gate_ref[:, span], preferred_element_type=jnp.float32)
        up = jnp.dot(normed, up_ref[:, span], preferred_element_type=jnp.float32)
        hidden_ref[:, span] = (gate / (1.0 + jnp.exp(-gate)) * up).astype(jnp.bfloat16)
    hidden = hidden_ref[...]
    step = min(512, features)
    for at in range(0, features, step):
        span = slice(at, at + step)
        part = jnp.dot(hidden, down_ref[:, span], preferred_element_type=jnp.float32)
        part = part.astype(jnp.bfloat16)
        for j in range(count):
            outs[j][:, span] = part[j * size : (j + 1) * size]


def combine_kernel(base_ref, high_ref, low_ref, *refs):
    blocks, out_ref = refs[:-1], refs[-1]
    high, low = high_ref[...], low_ref[...]
    step = min(512, base_ref.shape[1])
    for at in range(0, base_ref.shape[1], step):
        span = slice(at, at + step)
        values = jnp.concatenate([ref[:, span] for ref in blocks], axis=0)
        total = base_ref[:, span].astype(jnp.float32)
        total += jnp.dot(high, values, preferred_element_type=jnp.float32)
        total += jnp.dot(low, values, preferred_element_type=jnp.float32)
        out_ref[:, span] = total.astype(out_ref.dtype)


def stack_kernel(count, start, size, *refs):
    out_ref = refs[-1]
    for k in range(count):
        out_ref[k * size : (k + 1) * size] = refs[k][start : start + size]


SMEM = pl.BlockSpec(memory_space=pltpu.SMEM)
VMEM = pl.BlockSpec(memory_space=pltpu.VMEM)
HBM = pl.BlockSpec(memory_space=pltpu.HBM)
ANY = pl.BlockSpec(memory_space=pl.ANY)
CHEAP = pl.CostEstimate(flops=1, bytes_accessed=1, transcendentals=0)
PARAMS = pltpu.CompilerParams(vmem_limit_bytes=20 * 1024 * 1024)


def load(*arrays):
    return pl.pallas_call(
        load_kernel,
        in_specs=[HBM] * len(arrays),
        out_specs=[VMEM] * len(arrays),
        out_shape=[pltpu.VMEM(array.shape, array.dtype) for array in arrays],
        scratch_shapes=[pltpu.SemaphoreType.DMA((len(arrays),))],
        compiler_params=pltpu.CompilerParams(vmem_limit_bytes=1024 * 1024),
        cost_estimate=CHEAP,
        name="load",
    )(*[pltpu.with_memory_space_constraint(array, pltpu.HBM) for array in arrays])


def stacked(blocks, start, size, after=()):
    return pl.pallas_call(
        functools.partial(stack_kernel, len(blocks), start, size),
        in_specs=[VMEM] * len(blocks) + [ANY] * len(after),
        out_specs=VMEM,
        out_shape=jax.ShapeDtypeStruct((len(blocks) * size, blocks[0].shape[1]), blocks[0].dtype),
        compiler_params=PARAMS,
        cost_estimate=CHEAP,
        name="stack",
    )(*blocks, *after)


def combine(base, high, low, blocks, dtype):
    return pl.pallas_call(
        combine_kernel,
        in_specs=[VMEM] * (3 + len(blocks)),
        out_specs=VMEM,
        out_shape=jax.ShapeDtypeStruct(base.shape, dtype),
        compiler_params=PARAMS,
        cost_estimate=CHEAP,
        name="combine",
    )(base, high.T, low.T, *blocks)


def run_experts(blocks, size, gain, gate, up, down, after=()):
    count, features = len(blocks), blocks[0].shape[1]
    rows, units = count * size, gate.shape[1]
    return pl.pallas_call(
        functools.partial(expert_kernel, count, size),
        in_specs=[VMEM] * (count + 4) + [ANY] * len(after),
        out_specs=[VMEM] * count,
        out_shape=[jax.ShapeDtypeStruct((size, features), jnp.bfloat16)] * count,
        scratch_shapes=[
            pltpu.VMEM((rows, features), jnp.bfloat16),
            pltpu.VMEM((rows, units), jnp.bfloat16),
        ],
        compiler_params=PARAMS,
        cost_estimate=CHEAP,
        name="experts",
    )(*blocks, gain, gate, up, down, *after)


def shards(tokens, routes, norm_gain, router, gate_weight, up_weight, down_weight):
    batches, count, features = tokens.shape[1:]
    experts = router.shape[2]
    width = lax.axis_size("expert")
    groups, size = width // experts, batches * CAP
    flips = tuple(range(width - 2, -1, -2))
    teams = [flips[len(flips) // 2 :], flips[: len(flips) // 2]]
    flips = teams[0] + teams[1]
    rows = tokens.reshape(batches * count, features)
    chosen = jnp.swapaxes(routes[0, 0], 1, 2)
    me = lax.axis_index("expert").astype(jnp.int32).reshape(1)

    other_rows, other_chosen = moved(rows, 0, 1), moved(chosen, 0, 1)
    held_rows, held_chosen = load(rows, chosen)
    outgoing = pl.pallas_call(
        functools.partial(pack_kernel, width, groups, flips, size),
        in_specs=[SMEM] + [VMEM] * 4,
        out_specs=[VMEM] * len(flips),
        out_shape=[jax.ShapeDtypeStruct((2 * size, features), jnp.bfloat16)] * len(flips),
        compiler_params=PARAMS,
        cost_estimate=CHEAP,
        name="pack",
    )(me, held_chosen, other_chosen, held_rows, other_rows)
    arrived = [moved(block, 1, i) for block, i in zip(outgoing, flips)]

    held = load(gate_weight[0], up_weight[0], down_weight[0])
    first = len(teams[0])
    out = list(run_experts(arrived[:first], 2 * size, norm_gain, *held))
    out += run_experts(arrived[first:], 2 * size, norm_gain, *held, after=out[:1])
    spare = -(experts + 1) % 16
    extra = [router[0].T, norm_gain, jnp.zeros((spare, features), jnp.bfloat16)]
    out[first - 1] = jnp.concatenate([out[first - 1]] + extra, axis=0)
    returned = [moved(block, -1, i) for block, i in zip(out, flips)]
    there = returned[first - 1][2 * size :]

    weights = pl.pallas_call(
        functools.partial(weight_kernel, width, groups, teams, size),
        in_specs=[SMEM, VMEM, VMEM, VMEM],
        out_specs=[VMEM] * 4,
        out_shape=[
            jax.ShapeDtypeStruct((2 * len(team) * size, batches * count), jnp.bfloat16)
            for _ in range(2)
            for team in teams
        ],
        compiler_params=PARAMS,
        cost_estimate=CHEAP,
        name="weights",
    )(me, chosen, rows, there)
    mine = [block[:size] for block in returned]
    mine += [moved(stacked(team, size, size), 0, 1) for team in (returned[:first], returned[first:])]
    high = jnp.concatenate(weights[0:2], axis=0)
    low = jnp.concatenate(weights[2:4], axis=0)
    mine = mine[:first] + [mine[-2]] + mine[first:-2] + [mine[-1]]
    return combine(rows, high, low, mine, jnp.bfloat16).reshape(tokens.shape)


def solution(mesh):
    placed = (
        P("section", None, "expert", None),
        P("section", None, None, "expert", None),
        P("section", None),
        P("section", None, None),
        P("section", None, "expert"),
        P("section", None, "expert"),
        P("section", "expert", None),
    )
    return jax.shard_map(
        shards,
        mesh=mesh,
        in_specs=placed,
        out_specs=P("section", None, "expert", None),
        check_vma=False,
    )
```

time: 104 us -> 80.8 us (0.78)
  the two profiles are of different devices: /device:TPU:0 before, /device:TPU:11 now
where the time goes in v2:
time: 80.8 us; the launch traced here: 80.7 us
  waiting for transfers between devices  50.3 us (62%)
  starting transfers between devices  15.8 us (20%)
  Pallas kernels  13.6 us (17%)
    ppermute x12, waiting for transfers between devices, moved(): return lax.ppermute(block, HOME, pairs)  50.3 us
    ppermute x12, starting transfers between devices, moved(): return lax.ppermute(block, HOME, pairs)  15.8 us
    pallas_call x2, Pallas kernels, load(): pl.pallas_call(load_kernel, in_specs=[HBM] * len(arrays), out_specs=[VMEM...  5.76 us
    pallas_call x2, Pallas kernels, run_experts(): pl.pallas_call(functools.partial(expert_kernel, count, size), in_specs=[V...  4.83 us
  transfers between devices with their start and end apart: 12, of which 7 were waited for; matrix products, arithmetic and copies ran while one was open for 1% of the time, Pallas kernels for 14%

profile of v2, /device:TPU:11, one launch (start us, length us, event | category | flops | bytes accessed | tf_op | source)
XLA Modules:
  0.0 80.7 jit_solution(17658720956758088940)
XLA Ops:
  0.0 0.7 collective-permute-start.1
  0.7 1.1 %load.2 = (bf16[128,2048]{1,0:T(8,128)(2,1)S(1)}, s32[2,2,64]{2,1,0:T(2,128)S(1)}) custom-call(bf16[128,2048]{1,0:T(8,128)(2,1)} %bitcast.17, s32[2,2,64]{2,1,0:T(2,128)} %bitcast.21), custom_call_target="tpu_custom_call" | custom-call | flops 1 | bytes 1 | tf_op jit(solution)/shard_map/load/pallas_call | solution.py:155
  1.8 0.7 collective-permute-done.refs_1_
  2.4 0.0 collective-permute-done.1.refs_3_
  2.4 1.0 %pack.1 = (bf16[80,2048]{1,0:T(8,128)(2,1)S(1)}, bf16[80,2048]{1,0:T(8,128)(2,1)S(1)}, bf16[80,2048]{1,0:T(8,128)(2,1)S(1)}, bf16[80,2048]{1,0:T(8,128)(2,1)S(1)}) custom-call(s32[1]{0:T(128)} %bitcast.1.me_ref, s32[2,2,64]{2,1,0:T(2,128)S(1)} %get-tuple-element.22.refs_0_, s32[2,2,64]{2,1,0:T(2,128)S(1)} %collective-permute-done.refs_1_, ...), custom_call_target="tpu_custom_call" | custom-call | flops 1 | bytes 1 | tf_op jit(solution)/shard_map/pack/pallas_call | solution.py:223
  3.4 1.1 %collective-permute-start.2 = (bf16[80,2048]{1,0:T(8,128)(2,1)S(1)}, bf16[80,2048]{1,0:T(8,128)(2,1)S(1)}, u32[]{:S(2)}, u32[]{:S(2)}) collective-permute-start(bf16[80,2048]{1,0:T(8,128)(2,1)S(1)} %get-tuple-element.24), channel_id=1, source_target_pairs={{0,10},{1,11},{2,8},{3,9},{4,14},{5,15},{6,12},{7,13},{8,18},{9,19... | collective-permute-start | bytes 983048 | tf_op jit(solution)/shard_map/ppermute | solution.py:22
  4.6 1.2 %collective-permute-start.3 = (bf16[80,2048]{1,0:T(8,128)(2,1)S(1)}, bf16[80,2048]{1,0:T(8,128)(2,1)S(1)}, u32[]{:S(2)}, u32[]{:S(2)}) collective-permute-start(bf16[80,2048]{1,0:T(8,128)(2,1)S(1)} %get-tuple-element.25), channel_id=1, source_target_pairs={{0,8},{1,9},{2,10},{3,11},{4,12},{5,13},{6,14},{7,15},{8,16},{9,17... | collective-permute-start | bytes 983048 | tf_op jit(solution)/shard_map/ppermute | solution.py:22
  5.8 4.7 %load.3 = (bf16[2048,1024]{1,0:T(8,128)(2,1)S(1)}, bf16[2048,1024]{1,0:T(8,128)(2,1)S(1)}, bf16[1024,2048]{1,0:T(8,128)(2,1)S(1)}) custom-call(bf16[2048,1024]{1,0:T(8,128)(2,1)} %bitcast.23, bf16[2048,1024]{1,0:T(8,128)(2,1)} %bitcast.24, bf16[1024,2048]{1,0:T(8,128)(2,1)} %bitcast.25), custom_call_target="tpu_custom_call" | custom-call | flops 1 | bytes 1 | tf_op jit(solution)/shard_map/load/pallas_call | solution.py:155
  10.5 0.1 pad.7.clone
  10.6 2.3 %collective-permute-start.7 = (bf16[80,2048]{1,0:T(8,128)(2,1)S(1)}, bf16[80,2048]{1,0:T(8,128)(2,1)S(1)}, u32[]{:S(2)}, u32[]{:S(2)}) collective-permute-start(bf16[80,2048]{1,0:T(8,128)(2,1)S(1)} %get-tuple-element.35), channel_id=1, source_target_pairs={{0,14},{1,15},{2,12},{3,13},{4,10},{5,11},{6,8},{7,9},{8,22},{9,23... | collective-permute-start | bytes 983048 | tf_op jit(solution)/shard_map/ppermute | solution.py:22
  12.9 1.9 %collective-permute-start.8 = (bf16[80,2048]{1,0:T(8,128)(2,1)S(1)}, bf16[80,2048]{1,0:T(8,128)(2,1)S(1)}, u32[]{:S(2)}, u32[]{:S(2)}) collective-permute-start(bf16[80,2048]{1,0:T(8,128)(2,1)S(1)} %get-tuple-element.36), channel_id=1, source_target_pairs={{0,12},{1,13},{2,14},{3,15},{4,8},{5,9},{6,10},{7,11},{8,20},{9,21... | collective-permute-start | bytes 983048 | tf_op jit(solution)/shard_map/ppermute | solution.py:22
  14.8 9.4 %collective-permute-done.3.refs_1_ = bf16[80,2048]{1,0:T(8,128)(2,1)S(1)} collective-permute-done((bf16[80,2048]{1,0:T(8,128)(2,1)S(1)}, bf16[80,2048]{1,0:T(8,128)(2,1)S(1)}, u32[]{:S(2)}, u32[]{:S(2)}) %collective-permute-start.3) | collective-permute-done | bytes 327712 | tf_op jit(solution)/shard_map/ppermute | solution.py:22
  24.2 2.4 %experts.2 = (bf16[80,2048]{1,0:T(8,128)(2,1)S(1)}, bf16[80,2048]{1,0:T(8,128)(2,1)S(1)}) custom-call(bf16[80,2048]{1,0:T(8,128)(2,1)S(1)} %collective-permute-done.2.refs_0_, bf16[80,2048]{1,0:T(8,128)(2,1)S(1)} %collective-permute-done.3.refs_1_, bf16[1,2048]{1,0:T(2,128)(2,1)S(1)} %copy-done.1, bf16[2048,1024]{1,0:T(8,128)(2,1)S(1)} %get-tuple-element.26.refs_3_, ...), custom_call_target="tpu_custom_call" | custom-call | flops 1 | bytes 1 | tf_op jit(solution)/shard_map/experts/pallas_call | solution.py:194
  26.6 0.1 maximum_maximum_fusion
  26.8 1.2 %collective-permute-start.4 = (bf16[96,2048]{1,0:T(8,128)(2,1)S(1)}, bf16[96,2048]{1,0:T(8,128)(2,1)S(1)}, u32[]{:S(2)}, u32[]{:S(2)}) collective-permute-start(bf16[96,2048]{1,0:T(8,128)(2,1)S(1)} %maximum_maximum_fusion), channel_id=1, source_target_pairs={{0,24},{1,25},{2,26},{3,27},{4,28},{5,29},{6,30},{7,31},{8,0},{9,1... | collective-permute-start | bytes 1179656 | tf_op jit(solution)/shard_map/ppermute | solution.py:22
  28.0 6.0 %collective-permute-done.7.refs_0_ = bf16[80,2048]{1,0:T(8,128)(2,1)S(1)} collective-permute-done((bf16[80,2048]{1,0:T(8,128)(2,1)S(1)}, bf16[80,2048]{1,0:T(8,128)(2,1)S(1)}, u32[]{:S(2)}, u32[]{:S(2)}) %collective-permute-start.7) | collective-permute-done | bytes 327712 | tf_op jit(solution)/shard_map/ppermute | solution.py:22
  33.9 6.7 %collective-permute-done.8.refs_1_ = bf16[80,2048]{1,0:T(8,128)(2,1)S(1)} collective-permute-done((bf16[80,2048]{1,0:T(8,128)(2,1)S(1)}, bf16[80,2048]{1,0:T(8,128)(2,1)S(1)}, u32[]{:S(2)}, u32[]{:S(2)}) %collective-permute-start.8) | collective-permute-done | bytes 327712 | tf_op jit(solution)/shard_map/ppermute | solution.py:22
  40.6 2.4 %experts.3 = (bf16[80,2048]{1,0:T(8,128)(2,1)S(1)}, bf16[80,2048]{1,0:T(8,128)(2,1)S(1)}) custom-call(bf16[80,2048]{1,0:T(8,128)(2,1)S(1)} %collective-permute-done.7.refs_0_, bf16[80,2048]{1,0:T(8,128)(2,1)S(1)} %collective-permute-done.8.refs_1_, bf16[1,2048]{1,0:T(2,128)(2,1)S(1)} %copy-done.1, bf16[2048,1024]{1,0:T(8,128)(2,1)S(1)} %get-tuple-element.26.refs_3_, ...), custom_call_target="tpu_custom_call" | custom-call | flops 1 | bytes 1 | tf_op jit(solution)/shard_map/experts/pallas_call | solution.py:194
  43.1 5.0 %collective-permute-start.10 = (bf16[80,2048]{1,0:T(8,128)(2,1)S(1)}, bf16[80,2048]{1,0:T(8,128)(2,1)S(1)}, u32[]{:S(2)}, u32[]{:S(2)}) collective-permute-start(bf16[80,2048]{1,0:T(8,128)(2,1)S(1)} %get-tuple-element.38), channel_id=1, source_target_pairs={{0,28},{1,29},{2,30},{3,31},{4,24},{5,25},{6,26},{7,27},{8,4},{9,5... | collective-permute-start | bytes 983048 | tf_op jit(solution)/shard_map/ppermute | solution.py:22
  48.1 1.2 %collective-permute-start.5 = (bf16[80,2048]{1,0:T(8,128)(2,1)S(1)}, bf16[80,2048]{1,0:T(8,128)(2,1)S(1)}, u32[]{:S(2)}, u32[]{:S(2)}) collective-permute-start(bf16[80,2048]{1,0:T(8,128)(2,1)S(1)} %get-tuple-element.34.refs_6_), channel_id=1, source_target_pairs={{0,26},{1,27},{2,24},{3,25},{4,30},{5,31},{6,28},{7,29},{8,2},{9,3... | collective-permute-start | bytes 983048 | tf_op jit(solution)/shard_map/ppermute | solution.py:22
  49.3 16.6 %collective-permute-done.10.refs_1_ = bf16[80,2048]{1,0:T(8,128)(2,1)S(1)} collective-permute-done((bf16[80,2048]{1,0:T(8,128)(2,1)S(1)}, bf16[80,2048]{1,0:T(8,128)(2,1)S(1)}, u32[]{:S(2)}, u32[]{:S(2)}) %collective-permute-start.10) | collective-permute-done | bytes 327712 | tf_op jit(solution)/shard_map/ppermute | solution.py:22
  65.9 10.5 %collective-permute-done.9.refs_0_ = bf16[80,2048]{1,0:T(8,128)(2,1)S(1)} collective-permute-done((bf16[80,2048]{1,0:T(8,128)(2,1)S(1)}, bf16[80,2048]{1,0:T(8,128)(2,1)S(1)}, u32[]{:S(2)}, u32[]{:S(2)}) %collective-permute-start.9) | collective-permute-done | bytes 327712 | tf_op jit(solution)/shard_map/ppermute | solution.py:22
  76.4 1.0 %collective-permute-start.11 = (bf16[80,2048]{1,0:T(8,128)(2,1)S(1)}, bf16[80,2048]{1,0:T(8,128)(2,1)S(1)}, u32[]{:S(2)}, u32[]{:S(2)}) collective-permute-start(bf16[80,2048]{1,0:T(8,128)(2,1)S(1)} %stack.3), channel_id=1, source_target_pairs={{0,1},{1,0},{2,3},{3,2},{4,5},{5,4},{6,7},{7,6},{8,9},{9,8},{10,11... | collective-permute-start | bytes 983048 | tf_op jit(solution)/shard_map/ppermute | solution.py:22
  77.5 0.1 collective-permute-start.6
  77.7 0.5 weights.1
  78.2 0.1 copy.10
  78.3 0.1 copy.11
  78.4 0.1 copy.8
  78.5 0.1 copy.9
  78.6 0.1 maximum_bitcast_fusion
  78.8 0.4 collective-permute-done.6.refs_2_
  79.2 1.5 %combine.1 = bf16[128,2048]{1,0:T(8,128)(2,1)} custom-call(bf16[128,2048]{1,0:T(8,128)(2,1)S(1)} %bitcast.19, bf16[128,320]{1,0:T(8,128)(2,1)S(1)} %get-tuple-element.39.high_ref, bf16[128,320]{1,0:T(8,128)(2,1)S(1)} %get-tuple-element.40.low_ref, bf16[40,2048]{1,0:T(8,128)(2,1)S(1)} %slice.21.refs_0_, bf16[40,2048]{1,0:T(8,128)(2,1)S(1)} %slice.22.refs_1_, ...), custom_call_target="tpu_custom_call" | custom-call | flops 1 | bytes 1 | tf_op jit(solution)/shard_map/combine/pallas_call | solution.py:180
  (22 shorter events, 0.1 us)
Async XLA Ops:
  0.0 2.4 %collective-permute-start.1 = (bf16[128,2048]{1,0:T(8,128)(2,1)}, bf16[128,2048]{1,0:T(8,128)(2,1)S(1)}, u32[]{:S(2)}, u32[]{:S(2)}) collective-permute-start(bf16[128,2048]{1,0:T(8,128)(2,1)} %bitcast.16), channel_id=1, source_target_pairs={{0,1},{1,0},{2,3},{3,2},{4,5},{5,4},{6,7},{7,6},{8,9},{9,8},{10,11... | collective-permute-start | bytes 1572872 | tf_op jit(solution)/shard_map/ppermute | solution.py:22
  0.7 1.8 %collective-permute-start = (s32[2,2,64]{2,1,0:T(2,128)}, s32[2,2,64]{2,1,0:T(2,128)S(1)}, u32[]{:S(2)}, u32[]{:S(2)}) collective-permute-start(s32[2,2,64]{2,1,0:T(2,128)} %bitcast.20), channel_id=1, source_target_pairs={{0,1},{1,0},{2,3},{3,2},{4,5},{5,4},{6,7},{7,6},{8,9},{9,8},{10,11... | collective-permute-start | bytes 3080 | tf_op jit(solution)/shard_map/ppermute | solution.py:22
  3.4 11.4 %collective-permute-start.2 = (bf16[80,2048]{1,0:T(8,128)(2,1)S(1)}, bf16[80,2048]{1,0:T(8,128)(2,1)S(1)}, u32[]{:S(2)}, u32[]{:S(2)}) collective-permute-start(bf16[80,2048]{1,0:T(8,128)(2,1)S(1)} %get-tuple-element.24), channel_id=1, source_target_pairs={{0,10},{1,11},{2,8},{3,9},{4,14},{5,15},{6,12},{7,13},{8,18},{9,19... | collective-permute-start | bytes 983048 | tf_op jit(solution)/shard_map/ppermute | solution.py:22
  4.6 19.6 %collective-permute-start.3 = (bf16[80,2048]{1,0:T(8,128)(2,1)S(1)}, bf16[80,2048]{1,0:T(8,128)(2,1)S(1)}, u32[]{:S(2)}, u32[]{:S(2)}) collective-permute-start(bf16[80,2048]{1,0:T(8,128)(2,1)S(1)} %get-tuple-element.25), channel_id=1, source_target_pairs={{0,8},{1,9},{2,10},{3,11},{4,12},{5,13},{6,14},{7,15},{8,16},{9,17... | collective-permute-start | bytes 983048 | tf_op jit(solution)/shard_map/ppermute | solution.py:22
  5.8 18.4 %copy-start.1 = (bf16[1,2048]{1,0:T(2,128)(2,1)S(1)}, bf16[1,2048]{1,0:T(2,128)(2,1)}, u32[]{:S(2)}) copy-start(bf16[1,2048]{1,0:T(2,128)(2,1)} %refs_2_.3) | copy-start | bytes 12292
  10.6 23.3 %collective-permute-start.7 = (bf16[80,2048]{1,0:T(8,128)(2,1)S(1)}, bf16[80,2048]{1,0:T(8,128)(2,1)S(1)}, u32[]{:S(2)}, u32[]{:S(2)}) collective-permute-start(bf16[80,2048]{1,0:T(8,128)(2,1)S(1)} %get-tuple-element.35), channel_id=1, source_target_pairs={{0,14},{1,15},{2,12},{3,13},{4,10},{5,11},{6,8},{7,9},{8,22},{9,23... | collective-permute-start | bytes 983048 | tf_op jit(solution)/shard_map/ppermute | solution.py:22
  12.9 27.7 %collective-permute-start.8 = (bf16[80,2048]{1,0:T(8,128)(2,1)S(1)}, bf16[80,2048]{1,0:T(8,128)(2,1)S(1)}, u32[]{:S(2)}, u32[]{:S(2)}) collective-permute-start(bf16[80,2048]{1,0:T(8,128)(2,1)S(1)} %get-tuple-element.36), channel_id=1, source_target_pairs={{0,12},{1,13},{2,14},{3,15},{4,8},{5,9},{6,10},{7,11},{8,20},{9,21... | collective-permute-start | bytes 983048 | tf_op jit(solution)/shard_map/ppermute | solution.py:22
  24.2 2.4 %copy-start.3 = (bf16[1,2048,8]{1,2,0:T(8,128)(2,1)S(1)}, bf16[1,2048,8]{1,2,0:T(8,128)(2,1)}, u32[]{:S(2)}) copy-start(bf16[1,2048,8]{1,2,0:T(8,128)(2,1)} %param.10) | copy-start | bytes 98308
  26.8 50.7 %collective-permute-start.4 = (bf16[96,2048]{1,0:T(8,128)(2,1)S(1)}, bf16[96,2048]{1,0:T(8,128)(2,1)S(1)}, u32[]{:S(2)}, u32[]{:S(2)}) collective-permute-start(bf16[96,2048]{1,0:T(8,128)(2,1)S(1)} %maximum_maximum_fusion), channel_id=1, source_target_pairs={{0,24},{1,25},{2,26},{3,27},{4,28},{5,29},{6,30},{7,31},{8,0},{9,1... | collective-permute-start | bytes 1179656 | tf_op jit(solution)/shard_map/ppermute | solution.py:22
  40.6 37.0 %copy-start = (bf16[1,2,64,2048]{3,2,1,0:T(8,128)(2,1)S(1)}, bf16[1,2,64,2048]{3,2,1,0:T(8,128)(2,1)}, u32[]{:S(2)}) copy-start(bf16[1,2,64,2048]{3,2,1,0:T(8,128)(2,1)} %param.7) | copy-start | bytes 1572868
  40.6 37.0 %copy-start.2 = (s32[1,1,2,64,2]{3,4,2,1,0:T(2,128)S(1)}, s32[1,1,2,64,2]{3,4,2,1,0:T(2,128)}, u32[]{:S(2)}) copy-start(s32[1,1,2,64,2]{3,4,2,1,0:T(2,128)} %param.8) | copy-start | bytes 3076
  43.1 22.8 %collective-permute-start.10 = (bf16[80,2048]{1,0:T(8,128)(2,1)S(1)}, bf16[80,2048]{1,0:T(8,128)(2,1)S(1)}, u32[]{:S(2)}, u32[]{:S(2)}) collective-permute-start(bf16[80,2048]{1,0:T(8,128)(2,1)S(1)} %get-tuple-element.38), channel_id=1, source_target_pairs={{0,28},{1,29},{2,30},{3,31},{4,24},{5,25},{6,26},{7,27},{8,4},{9,5... | collective-permute-start | bytes 983048 | tf_op jit(solution)/shard_map/ppermute | solution.py:22
  48.1 28.3 %collective-permute-start.9 = (bf16[80,2048]{1,0:T(8,128)(2,1)S(1)}, bf16[80,2048]{1,0:T(8,128)(2,1)S(1)}, u32[]{:S(2)}, u32[]{:S(2)}) collective-permute-start(bf16[80,2048]{1,0:T(8,128)(2,1)S(1)} %get-tuple-element.37), channel_id=1, source_target_pairs={{0,30},{1,31},{2,28},{3,29},{4,26},{5,27},{6,24},{7,25},{8,6},{9,7... | collective-permute-start | bytes 983048 | tf_op jit(solution)/shard_map/ppermute | solution.py:22
  48.1 29.4 %collective-permute-start.5 = (bf16[80,2048]{1,0:T(8,128)(2,1)S(1)}, bf16[80,2048]{1,0:T(8,128)(2,1)S(1)}, u32[]{:S(2)}, u32[]{:S(2)}) collective-permute-start(bf16[80,2048]{1,0:T(8,128)(2,1)S(1)} %get-tuple-element.34.refs_6_), channel_id=1, source_target_pairs={{0,26},{1,27},{2,24},{3,25},{4,30},{5,31},{6,28},{7,29},{8,2},{9,3... | collective-permute-start | bytes 983048 | tf_op jit(solution)/shard_map/ppermute | solution.py:22
  76.4 2.3 %collective-permute-start.11 = (bf16[80,2048]{1,0:T(8,128)(2,1)S(1)}, bf16[80,2048]{1,0:T(8,128)(2,1)S(1)}, u32[]{:S(2)}, u32[]{:S(2)}) collective-permute-start(bf16[80,2048]{1,0:T(8,128)(2,1)S(1)} %stack.3), channel_id=1, source_target_pairs={{0,1},{1,0},{2,3},{3,2},{4,5},{5,4},{6,7},{7,6},{8,9},{9,8},{10,11... | collective-permute-start | bytes 983048 | tf_op jit(solution)/shard_map/ppermute | solution.py:22
  77.5 1.7 %collective-permute-start.6 = (bf16[80,2048]{1,0:T(8,128)(2,1)S(1)}, bf16[80,2048]{1,0:T(8,128)(2,1)S(1)}, u32[]{:S(2)}, u32[]{:S(2)}) collective-permute-start(bf16[80,2048]{1,0:T(8,128)(2,1)S(1)} %stack.2), channel_id=1, source_target_pairs={{0,1},{1,0},{2,3},{3,2},{4,5},{5,4},{6,7},{7,6},{8,9},{9,8},{10,11... | collective-permute-start | bytes 983048 | tf_op jit(solution)/shard_map/ppermute | solution.py:22

commit v3 on v2

v3 whole, which is shorter than its diff:
```python
import functools

import jax
import jax.numpy as jnp
from jax import lax
from jax.experimental import pallas as pl
from jax.experimental.pallas import tpu as pltpu
from jax.sharding import PartitionSpec as P

CAP = 20
epsilon = 1e-06
HOME = ("section", "expert")


def moved(block, by, flip):
    sections, width = lax.axis_size("section"), lax.axis_size("expert")
    pairs = [
        (s * width + e, (s + by) % sections * width + (e ^ flip))
        for s in range(sections)
        for e in range(width)
    ]
    return lax.ppermute(block, HOME, pairs)


def ranks(me, chosen, width, groups):
    tokens = chosen.shape[1]
    owner = lax.broadcasted_iota(jnp.int32, (width, tokens), 0) ^ me
    expert = owner // groups if groups > 1 else owner
    first = chosen[0:1, :] == expert
    match = first | (chosen[1:2, :] == expert)
    before = lax.broadcasted_iota(jnp.int32, (tokens, tokens), 0) < lax.broadcasted_iota(
        jnp.int32, (tokens, tokens), 1
    )
    rank = jnp.dot(
        match.astype(jnp.bfloat16), before.astype(jnp.bfloat16), preferred_element_type=jnp.float32
    ).astype(jnp.int32)
    return first, jnp.where(match, rank, -1)


def side_by_side(chosen_ref):
    return jnp.concatenate([chosen_ref[b] for b in range(chosen_ref.shape[0])], axis=1)


def pack_kernel(width, groups, flows, me_ref, *refs):
    chosen_refs, rows_refs, out_refs = refs[0:2], refs[2:4], refs[4:]
    for part in range(2):
        _, rank = ranks(me_ref[0], side_by_side(chosen_refs[part]), width, groups)
        rank = rank.astype(jnp.float32)
        select = []
        for flip, start, size in flows:
            place = lax.broadcasted_iota(jnp.int32, (size, rank.shape[1]), 0) + start
            select.append(jnp.where(rank[flip : flip + 1] == place.astype(jnp.float32), 1.0, 0.0))
        select = jnp.concatenate(select, axis=0).astype(jnp.bfloat16)
        packed = jnp.dot(select, rows_refs[part][...], preferred_element_type=jnp.float32)
        at = 0
        for out_ref, (_, _, size) in zip(out_refs, flows):
            out_ref[part * size : (part + 1) * size] = packed[at : at + size].astype(jnp.bfloat16)
            at += size


def weight_kernel(
    width, groups, order, me_ref, chosen_ref, rows_ref, there_ref, high_ref, low_ref
):
    chosen = side_by_side(chosen_ref)
    first, rank = ranks(me_ref[0], chosen, width, groups)
    experts = width // groups
    normed = normalised(rows_ref[...], there_ref[experts : experts + 1])
    logits = lax.dot_general(
        there_ref[0:experts], normed, (((1,), (1,)), ((), ())), preferred_element_type=jnp.float32
    )
    names = lax.broadcasted_iota(jnp.int32, logits.shape, 0)
    one = jnp.sum(jnp.where(names == chosen[0:1, :], logits, 0.0), axis=0, keepdims=True)
    two = jnp.sum(jnp.where(names == chosen[1:2, :], logits, 0.0), axis=0, keepdims=True)
    top = jnp.maximum(one, two)
    one, two = jnp.exp(one - top), jnp.exp(two - top)
    total = one + two
    weight = jnp.where(first, one / total, two / total)
    at = 0
    for flip, start, size in order:
        place = lax.broadcasted_iota(jnp.int32, (size, rank.shape[1]), 0) + start
        wide = jnp.where(rank[flip : flip + 1] == place, weight[flip : flip + 1], 0.0)
        high = wide.astype(jnp.bfloat16)
        high_ref[at : at + size] = high
        low_ref[at : at + size] = (wide - high.astype(jnp.float32)).astype(jnp.bfloat16)
        at += size


def normalised(rows, gain):
    wide = rows.astype(jnp.float32)
    scale = lax.rsqrt(jnp.mean(wide * wide, axis=-1, keepdims=True) + epsilon)
    return (wide * scale * gain.astype(jnp.float32)).astype(jnp.bfloat16)


def load_kernel(count, *refs):
    sources, held, sems = refs[:count], refs[-1 - count : -1], refs[-1]
    copies = [
        pltpu.make_async_copy(source, place, sems.at[k])
        for k, (source, place) in enumerate(zip(sources, held))
    ]
    for copy in copies:
        copy.start()
    for copy in copies:
        copy.wait()


def expert_kernel(sizes, ride, *refs):
    count = len(sizes)
    blocks, (gain_ref, router_ref), (gate_ref, up_ref, down_ref) = (
        refs[:count],
        refs[count : count + 2],
        refs[count + 2 : count + 5],
    )
    outs, (normed_ref, hidden_ref) = refs[-2 - count : -2], refs[-2:]
    gain = gain_ref[...]
    units, features = down_ref.shape
    if ride is not None:
        experts, size = router_ref.shape[0], sizes[ride]
        outs[ride][size:] = jnp.zeros((outs[ride].shape[0] - size, features), jnp.bfloat16)
        outs[ride][size : size + experts] = router_ref[...]
        outs[ride][size + experts : size + experts + 1] = gain
    starts = [sum(sizes[:j]) for j in range(count)]
    for j in range(count):
        normed_ref[starts[j] : starts[j] + sizes[j]] = normalised(blocks[j][0 : sizes[j]], gain)
    normed = normed_ref[...]
    step = min(256, units)
    for at in range(0, units, step):
        span = slice(at, at + step)
        gate = jnp.dot(normed, gate_ref[:, span], preferred_element_type=jnp.float32)
        up = jnp.dot(normed, up_ref[:, span], preferred_element_type=jnp.float32)
        hidden_ref[:, span] = (gate / (1.0 + jnp.exp(-gate)) * up).astype(jnp.bfloat16)
    hidden = hidden_ref[...]
    step = min(512, features)
    for at in range(0, features, step):
        span = slice(at, at + step)
        part = jnp.dot(hidden, down_ref[:, span], preferred_element_type=jnp.float32)
        part = part.astype(jnp.bfloat16)
        for j in range(count):
            outs[j][0 : sizes[j], span] = part[starts[j] : starts[j] + sizes[j]]


def tiles(length, step):
    return [slice(at, at + step) for at in range(0, length, step)]


def combine_kernel(base_ref, high_ref, low_ref, *refs):
    blocks, out_ref = refs[:-1], refs[-1]
    high, low = high_ref[...], low_ref[...]
    step = min(512, base_ref.shape[1])
    for at in range(0, base_ref.shape[1], step):
        span = slice(at, at + step)
        values = jnp.concatenate([ref[:, span] for ref in blocks], axis=0)
        total = base_ref[:, span].astype(jnp.float32)
        total += jnp.dot(high, values, preferred_element_type=jnp.float32)
        total += jnp.dot(low, values, preferred_element_type=jnp.float32)
        out_ref[:, span] = total.astype(out_ref.dtype)


def final_kernel(base_ref, high_ref, low_ref, values_ref, out_ref, done_ref, sems):
    high, low = high_ref[...], low_ref[...]
    copies = []
    for at, span in enumerate(tiles(base_ref.shape[1], min(512, base_ref.shape[1]))):
        values = values_ref[:, span]
        total = base_ref[:, span]
        total += jnp.dot(high, values, preferred_element_type=jnp.float32)
        total += jnp.dot(low, values, preferred_element_type=jnp.float32)
        done_ref[:, span] = total.astype(done_ref.dtype)
        copies.append(pltpu.make_async_copy(done_ref.at[:, span], out_ref.at[:, span], sems.at[at]))
        copies[-1].start()
    for copy in copies:
        copy.wait()


def stack_kernel(sizes, *refs):
    out_ref, at = refs[-1], 0
    for ref, size in zip(refs, sizes):
        out_ref[at : at + size] = ref[size : 2 * size]
        at += size


SMEM = pl.BlockSpec(memory_space=pltpu.SMEM)
VMEM = pl.BlockSpec(memory_space=pltpu.VMEM)
HBM = pl.BlockSpec(memory_space=pltpu.HBM)
ANY = pl.BlockSpec(memory_space=pl.ANY)
CHEAP = pl.CostEstimate(flops=1, bytes_accessed=1, transcendentals=0)
PARAMS = pltpu.CompilerParams(vmem_limit_bytes=20 * 1024 * 1024)


def load(*arrays):
    return pl.pallas_call(
        functools.partial(load_kernel, len(arrays)),
        in_specs=[HBM] * len(arrays),
        out_specs=[VMEM] * len(arrays),
        out_shape=[pltpu.VMEM(array.shape, array.dtype) for array in arrays],
        scratch_shapes=[pltpu.SemaphoreType.DMA((len(arrays),))],
        compiler_params=pltpu.CompilerParams(vmem_limit_bytes=1024 * 1024),
        cost_estimate=CHEAP,
        name="load",
    )(*[pltpu.with_memory_space_constraint(array, pltpu.HBM) for array in arrays])


def stacked(blocks, sizes):
    return pl.pallas_call(
        functools.partial(stack_kernel, sizes),
        in_specs=[VMEM] * len(blocks),
        out_specs=VMEM,
        out_shape=jax.ShapeDtypeStruct((sum(sizes), blocks[0].shape[1]), blocks[0].dtype),
        compiler_params=PARAMS,
        cost_estimate=CHEAP,
        name="stack",
    )(*blocks)


def finish(base, high, low, values):
    rows, features = base.shape
    return pl.pallas_call(
        final_kernel,
        in_specs=[VMEM] * 4,
        out_specs=HBM,
        out_shape=jax.ShapeDtypeStruct((rows, features), jnp.bfloat16),
        scratch_shapes=[
            pltpu.VMEM((rows, features), jnp.bfloat16),
            pltpu.SemaphoreType.DMA((len(tiles(features, min(512, features))),)),
        ],
        compiler_params=PARAMS,
        cost_estimate=CHEAP,
        name="finish",
    )(base, high.T, low.T, values)


def combine(base, high, low, blocks):
    return pl.pallas_call(
        combine_kernel,
        in_specs=[VMEM] * (3 + len(blocks)),
        out_specs=VMEM,
        out_shape=jax.ShapeDtypeStruct(base.shape, jnp.float32),
        compiler_params=PARAMS,
        cost_estimate=CHEAP,
        name="combine",
    )(base, high.T, low.T, *blocks)


def run_experts(blocks, sizes, ride, gain, router, held, after=()):
    count, features = len(blocks), gain.shape[1]
    rows, units = sum(sizes), held[0].shape[1]
    spare = -(-(router.shape[0] + 1) // 16) * 16
    return pl.pallas_call(
        functools.partial(expert_kernel, tuple(sizes), ride),
        in_specs=[VMEM] * (count + 5) + [ANY] * len(after),
        out_specs=[VMEM] * count,
        out_shape=[
            jax.ShapeDtypeStruct((size + (spare if j == ride else 0), features), jnp.bfloat16)
            for j, size in enumerate(sizes)
        ],
        scratch_shapes=[
            pltpu.VMEM((rows, features), jnp.bfloat16),
            pltpu.VMEM((rows, units), jnp.bfloat16),
        ],
        compiler_params=PARAMS,
        cost_estimate=CHEAP,
        name="experts",
    )(*blocks, gain, router, *held, *after)


FLOWS = ((3, 0, 16), (2, 0, 16), (1, 0, None), (0, 0, None), (3, 16, None), (2, 16, None))
TEAMS = ((0, 1, 3), (2,), (4, 5))
BACK = (0, 1, 4, 5, 2, 3)
RIDER = 3


def shards(tokens, routes, norm_gain, router, gate_weight, up_weight, down_weight):
    batches, count, features = tokens.shape[1:]
    experts = router.shape[2]
    width = lax.axis_size("expert")
    groups, size = width // experts, batches * CAP
    quarter = width // 4
    flows, members = [], []
    for band, start, stop in FLOWS:
        members.append([])
        for flip in range((band + 1) * quarter - 2, band * quarter - 1, -2):
            members[-1].append(len(flows))
            flows.append((flip, start, (size if stop is None else stop) - start))
    pick = lambda bands: [f for band in bands for f in members[band]]
    sizes = [2 * flow[2] for flow in flows]
    rows = tokens.reshape(batches * count, features)
    chosen = jnp.swapaxes(routes[0, 0], 1, 2)
    me = lax.axis_index("expert").astype(jnp.int32).reshape(1)

    other_rows, other_chosen = moved(rows, 0, 1), moved(chosen, 0, 1)
    held_rows, held_chosen = load(rows, chosen)
    outgoing = pl.pallas_call(
        functools.partial(pack_kernel, width, groups, flows),
        in_specs=[SMEM] + [VMEM] * 4,
        out_specs=[VMEM] * len(flows),
        out_shape=[jax.ShapeDtypeStruct((rows_of, features), jnp.bfloat16) for rows_of in sizes],
        compiler_params=PARAMS,
        cost_estimate=CHEAP,
        name="pack",
    )(me, held_chosen, other_chosen, held_rows, other_rows)
    arrived = [moved(block, 1, flow[0]) for block, flow in zip(outgoing, flows)]

    held = load(gate_weight[0], up_weight[0], down_weight[0])
    out, after = [None] * len(flows), []
    rider = pick([RIDER])[0]
    for team in TEAMS:
        mine = pick(team)
        results = run_experts(
            [arrived[f] for f in mine],
            [sizes[f] for f in mine],
            mine.index(rider) if rider in mine else None,
            norm_gain,
            router[0].T,
            held,
            after,
        )
        for f, result in zip(mine, results):
            out[f] = result
        after = [results[0]]
    returned = [None] * len(flows)
    for f in pick(BACK):
        returned[f] = moved(out[f], -1, flows[f][0])

    order = list(flows) + [(flip + 1, start, count) for flip, start, count in flows]
    high, low = pl.pallas_call(
        functools.partial(weight_kernel, width, groups, order),
        in_specs=[SMEM, VMEM, VMEM, VMEM],
        out_specs=[VMEM] * 2,
        out_shape=[jax.ShapeDtypeStruct((width * size, batches * count), jnp.bfloat16)] * 2,
        compiler_params=PARAMS,
        cost_estimate=CHEAP,
        name="weights",
    )(me, held_chosen, held_rows, returned[rider][sizes[rider] :])
    passed = moved(stacked(returned, [flow[2] for flow in flows]), 0, 1)
    own = [block[: flow[2]] for block, flow in zip(returned, flows)]
    half = width * size // 2
    total = combine(held_rows, high[:half], low[:half], own)
    return finish(total, high[half:], low[half:], passed).reshape(tokens.shape)


def solution(mesh):
    placed = (
        P("section", None, "expert", None),
        P("section", None, None, "expert", None),
        P("section", None),
        P("section", None, None),
        P("section", None, "expert"),
        P("section", None, "expert"),
        P("section", "expert", None),
    )
    return jax.shard_map(
        shards,
        mesh=mesh,
        in_specs=placed,
        out_specs=P("section", None, "expert", None),
        check_vma=False,
    )
```

time: 80.8 us -> 74.5 us (0.922)
  the two profiles are of different devices: /device:TPU:11 before, /device:TPU:0 now
where the time goes in v3:
time: 74.5 us; the launch traced here: 74.3 us
  starting transfers between devices  42.2 us (57%)
  waiting for transfers between devices  16 us (21%)
  Pallas kernels  15.5 us (21%)
    ppermute x15, starting transfers between devices, moved(): return lax.ppermute(block, HOME, pairs)  42.2 us
    ppermute x15, waiting for transfers between devices, moved(): return lax.ppermute(block, HOME, pairs)  16 us
    pallas_call x3, Pallas kernels, run_experts(): pl.pallas_call(functools.partial(expert_kernel, tuple(sizes), ride), in_s...  6.93 us
    pallas_call x2, Pallas kernels, load(): pl.pallas_call(functools.partial(load_kernel, len(arrays)), in_specs=[HBM...  5.75 us
  transfers between devices with their start and end apart: 15, of which 7 were waited for; matrix products, arithmetic and copies ran while one was open for 1% of the time, Pallas kernels for 18%

profile of v3, /device:TPU:0, one launch (start us, length us, event | category | flops | bytes accessed | tf_op | source)
XLA Modules:
  0.0 74.3 jit_solution(15803673724980657877)
XLA Ops:
  0.0 0.5 collective-permute-start.1
  0.5 0.1 collective-permute-start
  0.5 1.1 %load.2 = (bf16[128,2048]{1,0:T(8,128)(2,1)S(1)}, s32[2,2,64]{2,1,0:T(2,128)S(1)}) custom-call(bf16[128,2048]{1,0:T(8,128)(2,1)} %bitcast.27, s32[2,2,64]{2,1,0:T(2,128)} %bitcast.29), custom_call_target="tpu_custom_call" | custom-call | flops 1 | bytes 1 | tf_op jit(solution)/shard_map/load/pallas_call | solution.py:189
  1.6 0.6 collective-permute-done.refs_1_
  2.2 0.8 %pack.1 = (bf16[32,2048]{1,0:T(8,128)(2,1)S(1)}, bf16[32,2048]{1,0:T(8,128)(2,1)S(1)}, bf16[80,2048]{1,0:T(8,128)(2,1)S(1)}, bf16[80,2048]{1,0:T(8,128)(2,1)S(1)...) custom-call(s32[1]{0:T(128)} %bitcast.3.me_ref, s32[2,2,64]{2,1,0:T(2,128)S(1)} %get-tuple-element.24.refs_0_.chosen_ref, ...), custom_call_target="tpu_custom_call" | custom-call | flops 1 | bytes 1 | tf_op jit(solution)/shard_map/pack/pallas_call | solution.py:290
  3.0 2.9 %collective-permute-start.4 = (bf16[80,2048]{1,0:T(8,128)(2,1)S(1)}, bf16[80,2048]{1,0:T(8,128)(2,1)S(1)}, u32[]{:S(2)}, u32[]{:S(2)}) collective-permute-start(bf16[80,2048]{1,0:T(8,128)(2,1)S(1)} %get-tuple-element.27), channel_id=1, source_target_pairs={{0,8},{1,9},{2,10},{3,11},{4,12},{5,13},{6,14},{7,15},{8,16},{9,17... | collective-permute-start | bytes 983048 | tf_op jit(solution)/shard_map/ppermute | solution.py:22
  5.9 2.5 %collective-permute-start.8 = (bf16[80,2048]{1,0:T(8,128)(2,1)S(1)}, bf16[80,2048]{1,0:T(8,128)(2,1)S(1)}, u32[]{:S(2)}, u32[]{:S(2)}) collective-permute-start(bf16[80,2048]{1,0:T(8,128)(2,1)S(1)} %get-tuple-element.36), channel_id=1, source_target_pairs={{0,10},{1,11},{2,8},{3,9},{4,14},{5,15},{6,12},{7,13},{8,18},{9,19... | collective-permute-start | bytes 983048 | tf_op jit(solution)/shard_map/ppermute | solution.py:22
  8.4 3.4 %collective-permute-start.2 = (bf16[32,2048]{1,0:T(8,128)(2,1)S(1)}, bf16[32,2048]{1,0:T(8,128)(2,1)S(1)}, u32[]{:S(2)}, u32[]{:S(2)}) collective-permute-start(bf16[32,2048]{1,0:T(8,128)(2,1)S(1)} %get-tuple-element.25), channel_id=1, source_target_pairs={{0,14},{1,15},{2,12},{3,13},{4,10},{5,11},{6,8},{7,9},{8,22},{9,23... | collective-permute-start | bytes 393224 | tf_op jit(solution)/shard_map/ppermute | solution.py:22
  11.8 0.1 collective-permute-start.3
  11.9 4.7 %load.3 = (bf16[2048,1024]{1,0:T(8,128)(2,1)S(1)}, bf16[2048,1024]{1,0:T(8,128)(2,1)S(1)}, bf16[1024,2048]{1,0:T(8,128)(2,1)S(1)}) custom-call(bf16[2048,1024]{1,0:T(8,128)(2,1)} %bitcast.23, bf16[2048,1024]{1,0:T(8,128)(2,1)} %bitcast.24, bf16[1024,2048]{1,0:T(8,128)(2,1)} %bitcast.25), custom_call_target="tpu_custom_call" | custom-call | flops 1 | bytes 1 | tf_op jit(solution)/shard_map/load/pallas_call | solution.py:189
  16.6 3.8 %collective-permute-start.10 = (bf16[48,2048]{1,0:T(8,128)(2,1)S(1)}, bf16[48,2048]{1,0:T(8,128)(2,1)S(1)}, u32[]{:S(2)}, u32[]{:S(2)}) collective-permute-start(bf16[48,2048]{1,0:T(8,128)(2,1)S(1)} %get-tuple-element.37), channel_id=1, source_target_pairs={{0,14},{1,15},{2,12},{3,13},{4,10},{5,11},{6,8},{7,9},{8,22},{9,23... | collective-permute-start | bytes 589832 | tf_op jit(solution)/shard_map/ppermute | solution.py:22
  20.5 5.6 %collective-permute-done.2.refs_0_ = bf16[32,2048]{1,0:T(8,128)(2,1)S(1)} collective-permute-done((bf16[32,2048]{1,0:T(8,128)(2,1)S(1)}, bf16[32,2048]{1,0:T(8,128)(2,1)S(1)}, u32[]{:S(2)}, u32[]{:S(2)}) %collective-permute-start.2) | collective-permute-done | bytes 131104 | tf_op jit(solution)/shard_map/ppermute | solution.py:22
  26.1 2.3 %collective-permute-done.4.refs_2_ = bf16[80,2048]{1,0:T(8,128)(2,1)S(1)} collective-permute-done((bf16[80,2048]{1,0:T(8,128)(2,1)S(1)}, bf16[80,2048]{1,0:T(8,128)(2,1)S(1)}, u32[]{:S(2)}, u32[]{:S(2)}) %collective-permute-start.4) | collective-permute-done | bytes 327712 | tf_op jit(solution)/shard_map/ppermute | solution.py:22
  28.3 2.2 %experts.3 = (bf16[32,2048]{1,0:T(8,128)(2,1)S(1)}, bf16[32,2048]{1,0:T(8,128)(2,1)S(1)}, bf16[96,2048]{1,0:T(8,128)(2,1)S(1)}) custom-call(bf16[32,2048]{1,0:T(8,128)(2,1)S(1)} %collective-permute-done.2.refs_0_, bf16[32,2048]{1,0:T(8,128)(2,1)S(1)} %collective-permute-done.3.refs_1_, bf16[80,2048]{1,0:T(8,128)(2,1)S(1)} %collective-permute-done.4.refs_2_, ...), custom_call_target="tpu_custom_call" | custom-call | flops 1 | bytes 1 | tf_op jit(solution)/shard_map/experts/pallas_call | solution.py:246
  30.6 5.1 %collective-permute-start.5 = (bf16[96,2048]{1,0:T(8,128)(2,1)S(1)}, bf16[96,2048]{1,0:T(8,128)(2,1)S(1)}, u32[]{:S(2)}, u32[]{:S(2)}) collective-permute-start(bf16[96,2048]{1,0:T(8,128)(2,1)S(1)} %get-tuple-element.31), channel_id=1, source_target_pairs={{0,24},{1,25},{2,26},{3,27},{4,28},{5,29},{6,30},{7,31},{8,0},{9,1... | collective-permute-start | bytes 1179656 | tf_op jit(solution)/shard_map/ppermute | solution.py:22
  35.6 2.4 %experts.4.refs_7_ = bf16[80,2048]{1,0:T(8,128)(2,1)S(1)} custom-call(bf16[80,2048]{1,0:T(8,128)(2,1)S(1)} %collective-permute-done.8.refs_0_, bf16[1,2048]{1,0:T(2,128)(2,1)S(1)} %copy-done.1, bf16[8,2048]{1,0:T(8,128)(2,1)S(1)} %bitcast.21, bf16[2048,1024]{1,0:T(8,128)(2,1)S(1)} %get-tuple-element.28.refs_5_.refs_3_.refs_4_, ...), custom_call_target="tpu_custom_call" | custom-call | flops 1 | bytes 1 | tf_op jit(solution)/shard_map/experts/pallas_call | solution.py:246
  38.0 0.1 collective-permute-start.9
  38.1 5.1 %collective-permute-start.7 = (bf16[32,2048]{1,0:T(8,128)(2,1)S(1)}, bf16[32,2048]{1,0:T(8,128)(2,1)S(1)}, u32[]{:S(2)}, u32[]{:S(2)}) collective-permute-start(bf16[32,2048]{1,0:T(8,128)(2,1)S(1)} %get-tuple-element.35), channel_id=1, source_target_pairs={{0,28},{1,29},{2,30},{3,31},{4,24},{5,25},{6,26},{7,27},{8,4},{9,5... | collective-permute-start | bytes 393224 | tf_op jit(solution)/shard_map/ppermute | solution.py:22
  43.3 1.2 %collective-permute-done.11.refs_1_ = bf16[48,2048]{1,0:T(8,128)(2,1)S(1)} collective-permute-done((bf16[48,2048]{1,0:T(8,128)(2,1)S(1)}, bf16[48,2048]{1,0:T(8,128)(2,1)S(1)}, u32[]{:S(2)}, u32[]{:S(2)}) %collective-permute-start.11) | collective-permute-done | bytes 196640 | tf_op jit(solution)/shard_map/ppermute | solution.py:22
  44.4 2.3 %experts.5 = (bf16[48,2048]{1,0:T(8,128)(2,1)S(1)}, bf16[48,2048]{1,0:T(8,128)(2,1)S(1)}) custom-call(bf16[48,2048]{1,0:T(8,128)(2,1)S(1)} %collective-permute-done.10.refs_0_, bf16[48,2048]{1,0:T(8,128)(2,1)S(1)} %collective-permute-done.11.refs_1_, bf16[1,2048]{1,0:T(2,128)(2,1)S(1)} %copy-done.1, bf16[8,2048]{1,0:T(8,128)(2,1)S(1)} %bitcast.22, ...), custom_call_target="tpu_custom_call" | custom-call | flops 1 | bytes 1 | tf_op jit(solution)/shard_map/experts/pallas_call | solution.py:246
  46.7 1.7 %collective-permute-start.12 = (bf16[48,2048]{1,0:T(8,128)(2,1)S(1)}, bf16[48,2048]{1,0:T(8,128)(2,1)S(1)}, u32[]{:S(2)}, u32[]{:S(2)}) collective-permute-start(bf16[48,2048]{1,0:T(8,128)(2,1)S(1)} %get-tuple-element.39), channel_id=1, source_target_pairs={{0,30},{1,31},{2,28},{3,29},{4,26},{5,27},{6,24},{7,25},{8,6},{9,7... | collective-permute-start | bytes 589832 | tf_op jit(solution)/shard_map/ppermute | solution.py:22
  48.4 16.9 %collective-permute-start.6 = (bf16[32,2048]{1,0:T(8,128)(2,1)S(1)}, bf16[32,2048]{1,0:T(8,128)(2,1)S(1)}, u32[]{:S(2)}, u32[]{:S(2)}) collective-permute-start(bf16[32,2048]{1,0:T(8,128)(2,1)S(1)} %get-tuple-element.34.refs_6_), channel_id=1, source_target_pairs={{0,30},{1,31},{2,28},{3,29},{4,26},{5,27},{6,24},{7,25},{8,6},{9,7... | collective-permute-start | bytes 393224 | tf_op jit(solution)/shard_map/ppermute | solution.py:22
  65.3 2.5 %collective-permute-done.6.refs_0_ = bf16[32,2048]{1,0:T(8,128)(2,1)S(1)} collective-permute-done((bf16[32,2048]{1,0:T(8,128)(2,1)S(1)}, bf16[32,2048]{1,0:T(8,128)(2,1)S(1)}, u32[]{:S(2)}, u32[]{:S(2)}) %collective-permute-start.6) | collective-permute-done | bytes 131104 | tf_op jit(solution)/shard_map/ppermute | solution.py:22
  67.8 3.1 %collective-permute-done.13.refs_5_ = bf16[48,2048]{1,0:T(8,128)(2,1)S(1)} collective-permute-done((bf16[48,2048]{1,0:T(8,128)(2,1)S(1)}, bf16[48,2048]{1,0:T(8,128)(2,1)S(1)}, u32[]{:S(2)}, u32[]{:S(2)}) %collective-permute-start.13) | collective-permute-done | bytes 196640 | tf_op jit(solution)/shard_map/ppermute | solution.py:22
  71.0 0.1 collective-permute-start.14
  71.2 0.5 weights.1
  71.7 0.1 copy.8
  71.8 0.1 copy.9
  72.0 0.1 slice_bitcast_fusion
  72.1 0.4 combine.1.base_ref
  72.5 0.7 collective-permute-done.14.values_ref
  73.2 1.1 %finish.1 = bf16[128,2048]{1,0:T(8,128)(2,1)} custom-call(f32[128,2048]{1,0:T(8,128)S(1)} %combine.1.base_ref, bf16[128,160]{1,0:T(8,128)(2,1)S(1)} %get-tuple-element.46.high_ref, bf16[128,160]{1,0:T(8,128)(2,1)S(1)} %get-tuple-element.41.low_ref, bf16[160,2048]{1,0:T(8,128)(2,1)S(1)} %collective-permute-done.14.values_ref), custom_call_target="tpu_custom_call" | custom-call | flops 1 | bytes 1 | tf_op jit(solution)/shard_map/finish/pallas_call | solution.py:215
  (22 shorter events, 0.1 us)
Async XLA Ops:
  0.0 2.2 %collective-permute-start.1 = (bf16[128,2048]{1,0:T(8,128)(2,1)}, bf16[128,2048]{1,0:T(8,128)(2,1)S(1)}, u32[]{:S(2)}, u32[]{:S(2)}) collective-permute-start(bf16[128,2048]{1,0:T(8,128)(2,1)} %bitcast.26), channel_id=1, source_target_pairs={{0,1},{1,0},{2,3},{3,2},{4,5},{5,4},{6,7},{7,6},{8,9},{9,8},{10,11... | collective-permute-start | bytes 1572872 | tf_op jit(solution)/shard_map/ppermute | solution.py:22
  0.5 1.8 %collective-permute-start = (s32[2,2,64]{2,1,0:T(2,128)}, s32[2,2,64]{2,1,0:T(2,128)S(1)}, u32[]{:S(2)}, u32[]{:S(2)}) collective-permute-start(s32[2,2,64]{2,1,0:T(2,128)} %bitcast.28), channel_id=1, source_target_pairs={{0,1},{1,0},{2,3},{3,2},{4,5},{5,4},{6,7},{7,6},{8,9},{9,8},{10,11... | collective-permute-start | bytes 3080 | tf_op jit(solution)/shard_map/ppermute | solution.py:22
  3.0 25.3 %collective-permute-start.4 = (bf16[80,2048]{1,0:T(8,128)(2,1)S(1)}, bf16[80,2048]{1,0:T(8,128)(2,1)S(1)}, u32[]{:S(2)}, u32[]{:S(2)}) collective-permute-start(bf16[80,2048]{1,0:T(8,128)(2,1)S(1)} %get-tuple-element.27), channel_id=1, source_target_pairs={{0,8},{1,9},{2,10},{3,11},{4,12},{5,13},{6,14},{7,15},{8,16},{9,17... | collective-permute-start | bytes 983048 | tf_op jit(solution)/shard_map/ppermute | solution.py:22
  5.9 29.7 %collective-permute-start.8 = (bf16[80,2048]{1,0:T(8,128)(2,1)S(1)}, bf16[80,2048]{1,0:T(8,128)(2,1)S(1)}, u32[]{:S(2)}, u32[]{:S(2)}) collective-permute-start(bf16[80,2048]{1,0:T(8,128)(2,1)S(1)} %get-tuple-element.36), channel_id=1, source_target_pairs={{0,10},{1,11},{2,8},{3,9},{4,14},{5,15},{6,12},{7,13},{8,18},{9,19... | collective-permute-start | bytes 983048 | tf_op jit(solution)/shard_map/ppermute | solution.py:22
  8.4 17.6 %collective-permute-start.2 = (bf16[32,2048]{1,0:T(8,128)(2,1)S(1)}, bf16[32,2048]{1,0:T(8,128)(2,1)S(1)}, u32[]{:S(2)}, u32[]{:S(2)}) collective-permute-start(bf16[32,2048]{1,0:T(8,128)(2,1)S(1)} %get-tuple-element.25), channel_id=1, source_target_pairs={{0,14},{1,15},{2,12},{3,13},{4,10},{5,11},{6,8},{7,9},{8,22},{9,23... | collective-permute-start | bytes 393224 | tf_op jit(solution)/shard_map/ppermute | solution.py:22
  11.8 14.2 %collective-permute-start.3 = (bf16[32,2048]{1,0:T(8,128)(2,1)S(1)}, bf16[32,2048]{1,0:T(8,128)(2,1)S(1)}, u32[]{:S(2)}, u32[]{:S(2)}) collective-permute-start(bf16[32,2048]{1,0:T(8,128)(2,1)S(1)} %get-tuple-element.26), channel_id=1, source_target_pairs={{0,12},{1,13},{2,14},{3,15},{4,8},{5,9},{6,10},{7,11},{8,20},{9,21... | collective-permute-start | bytes 393224 | tf_op jit(solution)/shard_map/ppermute | solution.py:22
  11.9 16.4 %copy-start = (bf16[1,2048,8]{1,2,0:T(8,128)(2,1)S(1)}, bf16[1,2048,8]{1,2,0:T(8,128)(2,1)}, u32[]{:S(2)}) copy-start(bf16[1,2048,8]{1,2,0:T(8,128)(2,1)} %param.10) | copy-start | bytes 98308
  11.9 16.4 %copy-start.1 = (bf16[1,2048]{1,0:T(2,128)(2,1)S(1)}, bf16[1,2048]{1,0:T(2,128)(2,1)}, u32[]{:S(2)}) copy-start(bf16[1,2048]{1,0:T(2,128)(2,1)} %refs_2_.1) | copy-start | bytes 12292
  16.6 26.6 %collective-permute-start.10 = (bf16[48,2048]{1,0:T(8,128)(2,1)S(1)}, bf16[48,2048]{1,0:T(8,128)(2,1)S(1)}, u32[]{:S(2)}, u32[]{:S(2)}) collective-permute-start(bf16[48,2048]{1,0:T(8,128)(2,1)S(1)} %get-tuple-element.37), channel_id=1, source_target_pairs={{0,14},{1,15},{2,12},{3,13},{4,10},{5,11},{6,8},{7,9},{8,22},{9,23... | collective-permute-start | bytes 589832 | tf_op jit(solution)/shard_map/ppermute | solution.py:22
  26.1 18.4 %collective-permute-start.11 = (bf16[48,2048]{1,0:T(8,128)(2,1)S(1)}, bf16[48,2048]{1,0:T(8,128)(2,1)S(1)}, u32[]{:S(2)}, u32[]{:S(2)}) collective-permute-start(bf16[48,2048]{1,0:T(8,128)(2,1)S(1)} %get-tuple-element.38), channel_id=1, source_target_pairs={{0,12},{1,13},{2,14},{3,15},{4,8},{5,9},{6,10},{7,11},{8,20},{9,21... | collective-permute-start | bytes 589832 | tf_op jit(solution)/shard_map/ppermute | solution.py:22
  30.6 40.4 %collective-permute-start.5 = (bf16[96,2048]{1,0:T(8,128)(2,1)S(1)}, bf16[96,2048]{1,0:T(8,128)(2,1)S(1)}, u32[]{:S(2)}, u32[]{:S(2)}) collective-permute-start(bf16[96,2048]{1,0:T(8,128)(2,1)S(1)} %get-tuple-element.31), channel_id=1, source_target_pairs={{0,24},{1,25},{2,26},{3,27},{4,28},{5,29},{6,30},{7,31},{8,0},{9,1... | collective-permute-start | bytes 1179656 | tf_op jit(solution)/shard_map/ppermute | solution.py:22
  38.0 32.9 %collective-permute-start.9 = (bf16[80,2048]{1,0:T(8,128)(2,1)S(1)}, bf16[80,2048]{1,0:T(8,128)(2,1)S(1)}, u32[]{:S(2)}, u32[]{:S(2)}) collective-permute-start(bf16[80,2048]{1,0:T(8,128)(2,1)S(1)} %experts.4.refs_7_), channel_id=1, source_target_pairs={{0,26},{1,27},{2,24},{3,25},{4,30},{5,31},{6,28},{7,29},{8,2},{9,3... | collective-permute-start | bytes 983048 | tf_op jit(solution)/shard_map/ppermute | solution.py:22
  38.1 10.3 %collective-permute-start.7 = (bf16[32,2048]{1,0:T(8,128)(2,1)S(1)}, bf16[32,2048]{1,0:T(8,128)(2,1)S(1)}, u32[]{:S(2)}, u32[]{:S(2)}) collective-permute-start(bf16[32,2048]{1,0:T(8,128)(2,1)S(1)} %get-tuple-element.35), channel_id=1, source_target_pairs={{0,28},{1,29},{2,30},{3,31},{4,24},{5,25},{6,26},{7,27},{8,4},{9,5... | collective-permute-start | bytes 393224 | tf_op jit(solution)/shard_map/ppermute | solution.py:22
  46.7 21.1 %collective-permute-start.12 = (bf16[48,2048]{1,0:T(8,128)(2,1)S(1)}, bf16[48,2048]{1,0:T(8,128)(2,1)S(1)}, u32[]{:S(2)}, u32[]{:S(2)}) collective-permute-start(bf16[48,2048]{1,0:T(8,128)(2,1)S(1)} %get-tuple-element.39), channel_id=1, source_target_pairs={{0,30},{1,31},{2,28},{3,29},{4,26},{5,27},{6,24},{7,25},{8,6},{9,7... | collective-permute-start | bytes 589832 | tf_op jit(solution)/shard_map/ppermute | solution.py:22
  48.4 22.5 %collective-permute-start.13 = (bf16[48,2048]{1,0:T(8,128)(2,1)S(1)}, bf16[48,2048]{1,0:T(8,128)(2,1)S(1)}, u32[]{:S(2)}, u32[]{:S(2)}) collective-permute-start(bf16[48,2048]{1,0:T(8,128)(2,1)S(1)} %get-tuple-element.40), channel_id=1, source_target_pairs={{0,28},{1,29},{2,30},{3,31},{4,24},{5,25},{6,26},{7,27},{8,4},{9,5... | collective-permute-start | bytes 589832 | tf_op jit(solution)/shard_map/ppermute | solution.py:22
  48.4 19.4 %collective-permute-start.6 = (bf16[32,2048]{1,0:T(8,128)(2,1)S(1)}, bf16[32,2048]{1,0:T(8,128)(2,1)S(1)}, u32[]{:S(2)}, u32[]{:S(2)}) collective-permute-start(bf16[32,2048]{1,0:T(8,128)(2,1)S(1)} %get-tuple-element.34.refs_6_), channel_id=1, source_target_pairs={{0,30},{1,31},{2,28},{3,29},{4,26},{5,27},{6,24},{7,25},{8,6},{9,7... | collective-permute-start | bytes 393224 | tf_op jit(solution)/shard_map/ppermute | solution.py:22
  71.0 2.2 %collective-permute-start.14 = (bf16[160,2048]{1,0:T(8,128)(2,1)S(1)}, bf16[160,2048]{1,0:T(8,128)(2,1)S(1)}, u32[]{:S(2)}, u32[]{:S(2)}) collective-permute-start(bf16[160,2048]{1,0:T(8,128)(2,1)S(1)} %stack.1), channel_id=1, source_target_pairs={{0,1},{1,0},{2,3},{3,2},{4,5},{5,4},{6,7},{7,6},{8,9},{9,8},{10,11... | collective-permute-start | bytes 1966088 | tf_op jit(solution)/shard_map/ppermute | solution.py:22

commit v4 on v3

--- a/solution.py
+++ b/solution.py
@@ -155,11 +155,12 @@
         out_ref[:, span] = total.astype(out_ref.dtype)
 
 
-def final_kernel(base_ref, high_ref, low_ref, values_ref, out_ref, done_ref, sems):
+def final_kernel(base_ref, high_ref, low_ref, *refs):
+    blocks, (out_ref, done_ref, sems) = refs[:-3], refs[-3:]
     high, low = high_ref[...], low_ref[...]
     copies = []
     for at, span in enumerate(tiles(base_ref.shape[1], min(512, base_ref.shape[1]))):
-        values = values_ref[:, span]
+        values = jnp.concatenate([ref[:, span] for ref in blocks], axis=0)
         total = base_ref[:, span]
         total += jnp.dot(high, values, preferred_element_type=jnp.float32)
         total += jnp.dot(low, values, preferred_element_type=jnp.float32)
@@ -210,11 +211,11 @@
     )(*blocks)
 
 
-def finish(base, high, low, values):
+def finish(base, high, low, blocks):
     rows, features = base.shape
     return pl.pallas_call(
         final_kernel,
-        in_specs=[VMEM] * 4,
+        in_specs=[VMEM] * (3 + len(blocks)),
         out_specs=HBM,
         out_shape=jax.ShapeDtypeStruct((rows, features), jnp.bfloat16),
         scratch_shapes=[
@@ -224,7 +225,7 @@
         compiler_params=PARAMS,
         cost_estimate=CHEAP,
         name="finish",
-    )(base, high.T, low.T, values)
+    )(base, high.T, low.T, *blocks)
 
 
 def combine(base, high, low, blocks):
@@ -262,9 +263,10 @@
 
 
 FLOWS = ((3, 0, 16), (2, 0, 16), (1, 0, None), (0, 0, None), (3, 16, None), (2, 16, None))
-TEAMS = ((0, 1, 3), (2,), (4, 5))
+TEAMS = ((0, 3), (1, 2), (4, 5))
 BACK = (0, 1, 4, 5, 2, 3)
 RIDER = 3
+SWAPS = ((0, 1, 4, 5, 3), (2,))
 
 
 def shards(tokens, routes, norm_gain, router, gate_weight, up_weight, down_weight):
@@ -319,7 +321,9 @@
     for f in pick(BACK):
         returned[f] = moved(out[f], -1, flows[f][0])
 
-    order = list(flows) + [(flip + 1, start, count) for flip, start, count in flows]
+    early, late = pick(SWAPS[0]), pick(SWAPS[1])
+    order = [flows[f] for f in early + late]
+    order += [(flip + 1, start, taken) for flip, start, taken in order]
     high, low = pl.pallas_call(
         functools.partial(weight_kernel, width, groups, order),
         in_specs=[SMEM, VMEM, VMEM, VMEM],
@@ -329,11 +333,14 @@
         cost_estimate=CHEAP,
         name="weights",
     )(me, held_chosen, held_rows, returned[rider][sizes[rider] :])
-    passed = moved(stacked(returned, [flow[2] for flow in flows]), 0, 1)
-    own = [block[: flow[2]] for block, flow in zip(returned, flows)]
-    half = width * size // 2
-    total = combine(held_rows, high[:half], low[:half], own)
-    return finish(total, high[half:], low[half:], passed).reshape(tokens.shape)
+    mine = [[returned[f][: flows[f][2]] for f in part] for part in (early, late)]
+    passed = [
+        moved(stacked([returned[f] for f in part], [flows[f][2] for f in part]), 0, 1)
+        for part in (early, late)
+    ]
+    split = sum(block.shape[0] for block in mine[0])
+    total = combine(held_rows, high[:split], low[:split], mine[0])
+    return finish(total, high[split:], low[split:], mine[1] + passed).reshape(tokens.shape)
 
 
 def solution(mesh):

time: 74.5 us -> 74.1 us (level)
    ppermute x15 -> x16, starting transfers between devices: 42.2 us -> 41.6 us  [moved(): return lax.ppermute(block, HOME, pairs)]
    ppermute x15 -> x16, waiting for transfers between devices: 16 us -> 16.5 us  [moved(): return lax.ppermute(block, HOME, pairs)]
  transfers between devices with their start and end apart: 15 -> 16, of which waited for: 7 -> 7; matrix products, arithmetic and copies ran while one was open for 1% -> 1% of each run, Pallas kernels for 18% -> 18%
where the time goes in v4:
time: 74.1 us; the launch traced here: 73.9 us
  starting transfers between devices  41.6 us (56%)
  waiting for transfers between devices  16.5 us (22%)
  Pallas kernels  15.2 us (21%)
    ppermute x16, starting transfers between devices, moved(): return lax.ppermute(block, HOME, pairs)  41.6 us
    ppermute x16, waiting for transfers between devices, moved(): return lax.ppermute(block, HOME, pairs)  16.5 us
    pallas_call x3, Pallas kernels, run_experts(): pl.pallas_call(functools.partial(expert_kernel, tuple(sizes), ride), in_s...  6.64 us
    pallas_call x2, Pallas kernels, load(): pl.pallas_call(functools.partial(load_kernel, len(arrays)), in_specs=[HBM...  5.75 us
  transfers between devices with their start and end apart: 16, of which 7 were waited for; matrix products, arithmetic and copies ran while one was open for 1% of the time, Pallas kernels for 18%

profile of v4, /device:TPU:0, one launch (start us, length us, event | category | flops | bytes accessed | tf_op | source)
XLA Modules:
  0.0 73.9 jit_solution(14264312918350519597)
XLA Ops:
  0.0 0.5 collective-permute-start.1
  0.5 1.1 %load.2 = (bf16[128,2048]{1,0:T(8,128)(2,1)S(1)}, s32[2,2,64]{2,1,0:T(2,128)S(1)}) custom-call(bf16[128,2048]{1,0:T(8,128)(2,1)} %bitcast.27, s32[2,2,64]{2,1,0:T(2,128)} %bitcast.29), custom_call_target="tpu_custom_call" | custom-call | flops 1 | bytes 1 | tf_op jit(solution)/shard_map/load/pallas_call | solution.py:190
  1.6 0.6 collective-permute-done.refs_1_
  2.2 0.8 %pack.1 = (bf16[32,2048]{1,0:T(8,128)(2,1)S(1)}, bf16[32,2048]{1,0:T(8,128)(2,1)S(1)}, bf16[80,2048]{1,0:T(8,128)(2,1)S(1)}, bf16[80,2048]{1,0:T(8,128)(2,1)S(1)...) custom-call(s32[1]{0:T(128)} %bitcast.3.me_ref, s32[2,2,64]{2,1,0:T(2,128)S(1)} %get-tuple-element.25.refs_0_.chosen_ref, ...), custom_call_target="tpu_custom_call" | custom-call | flops 1 | bytes 1 | tf_op jit(solution)/shard_map/pack/pallas_call | solution.py:292
  3.0 2.9 %collective-permute-start.3 = (bf16[80,2048]{1,0:T(8,128)(2,1)S(1)}, bf16[80,2048]{1,0:T(8,128)(2,1)S(1)}, u32[]{:S(2)}, u32[]{:S(2)}) collective-permute-start(bf16[80,2048]{1,0:T(8,128)(2,1)S(1)} %get-tuple-element.27), channel_id=1, source_target_pairs={{0,8},{1,9},{2,10},{3,11},{4,12},{5,13},{6,14},{7,15},{8,16},{9,17... | collective-permute-start | bytes 983048 | tf_op jit(solution)/shard_map/ppermute | solution.py:22
  5.9 2.5 %collective-permute-start.7 = (bf16[80,2048]{1,0:T(8,128)(2,1)S(1)}, bf16[80,2048]{1,0:T(8,128)(2,1)S(1)}, u32[]{:S(2)}, u32[]{:S(2)}) collective-permute-start(bf16[80,2048]{1,0:T(8,128)(2,1)S(1)} %get-tuple-element.36), channel_id=1, source_target_pairs={{0,10},{1,11},{2,8},{3,9},{4,14},{5,15},{6,12},{7,13},{8,18},{9,19... | collective-permute-start | bytes 983048 | tf_op jit(solution)/shard_map/ppermute | solution.py:22
  8.4 3.4 %collective-permute-start.2 = (bf16[32,2048]{1,0:T(8,128)(2,1)S(1)}, bf16[32,2048]{1,0:T(8,128)(2,1)S(1)}, u32[]{:S(2)}, u32[]{:S(2)}) collective-permute-start(bf16[32,2048]{1,0:T(8,128)(2,1)S(1)} %get-tuple-element.26), channel_id=1, source_target_pairs={{0,14},{1,15},{2,12},{3,13},{4,10},{5,11},{6,8},{7,9},{8,22},{9,23... | collective-permute-start | bytes 393224 | tf_op jit(solution)/shard_map/ppermute | solution.py:22
  11.8 0.1 collective-permute-start.6
  11.9 4.7 %load.3 = (bf16[2048,1024]{1,0:T(8,128)(2,1)S(1)}, bf16[2048,1024]{1,0:T(8,128)(2,1)S(1)}, bf16[1024,2048]{1,0:T(8,128)(2,1)S(1)}) custom-call(bf16[2048,1024]{1,0:T(8,128)(2,1)} %bitcast.23, bf16[2048,1024]{1,0:T(8,128)(2,1)} %bitcast.24, bf16[1024,2048]{1,0:T(8,128)(2,1)} %bitcast.25), custom_call_target="tpu_custom_call" | custom-call | flops 1 | bytes 1 | tf_op jit(solution)/shard_map/load/pallas_call | solution.py:190
  16.6 3.8 %collective-permute-start.9 = (bf16[48,2048]{1,0:T(8,128)(2,1)S(1)}, bf16[48,2048]{1,0:T(8,128)(2,1)S(1)}, u32[]{:S(2)}, u32[]{:S(2)}) collective-permute-start(bf16[48,2048]{1,0:T(8,128)(2,1)S(1)} %get-tuple-element.38), channel_id=1, source_target_pairs={{0,14},{1,15},{2,12},{3,13},{4,10},{5,11},{6,8},{7,9},{8,22},{9,23... | collective-permute-start | bytes 589832 | tf_op jit(solution)/shard_map/ppermute | solution.py:22
  20.5 5.6 %collective-permute-done.2.refs_0_ = bf16[32,2048]{1,0:T(8,128)(2,1)S(1)} collective-permute-done((bf16[32,2048]{1,0:T(8,128)(2,1)S(1)}, bf16[32,2048]{1,0:T(8,128)(2,1)S(1)}, u32[]{:S(2)}, u32[]{:S(2)}) %collective-permute-start.2) | collective-permute-done | bytes 131104 | tf_op jit(solution)/shard_map/ppermute | solution.py:22
  26.1 2.3 %collective-permute-done.3.refs_1_ = bf16[80,2048]{1,0:T(8,128)(2,1)S(1)} collective-permute-done((bf16[80,2048]{1,0:T(8,128)(2,1)S(1)}, bf16[80,2048]{1,0:T(8,128)(2,1)S(1)}, u32[]{:S(2)}, u32[]{:S(2)}) %collective-permute-start.3) | collective-permute-done | bytes 327712 | tf_op jit(solution)/shard_map/ppermute | solution.py:22
  28.3 2.2 %experts.3 = (bf16[32,2048]{1,0:T(8,128)(2,1)S(1)}, bf16[96,2048]{1,0:T(8,128)(2,1)S(1)}) custom-call(bf16[32,2048]{1,0:T(8,128)(2,1)S(1)} %collective-permute-done.2.refs_0_, bf16[80,2048]{1,0:T(8,128)(2,1)S(1)} %collective-permute-done.3.refs_1_, bf16[1,2048]{1,0:T(2,128)(2,1)S(1)} %copy-done.1, bf16[8,2048]{1,0:T(8,128)(2,1)S(1)} %bitcast.20, ...), custom_call_target="tpu_custom_call" | custom-call | flops 1 | bytes 1 | tf_op jit(solution)/shard_map/experts/pallas_call | solution.py:247
  30.5 5.1 %collective-permute-start.4 = (bf16[96,2048]{1,0:T(8,128)(2,1)S(1)}, bf16[96,2048]{1,0:T(8,128)(2,1)S(1)}, u32[]{:S(2)}, u32[]{:S(2)}) collective-permute-start(bf16[96,2048]{1,0:T(8,128)(2,1)S(1)} %get-tuple-element.31), channel_id=1, source_target_pairs={{0,24},{1,25},{2,26},{3,27},{4,28},{5,29},{6,30},{7,31},{8,0},{9,1... | collective-permute-start | bytes 1179656 | tf_op jit(solution)/shard_map/ppermute | solution.py:22
  35.6 2.2 %experts.4 = (bf16[32,2048]{1,0:T(8,128)(2,1)S(1)}, bf16[80,2048]{1,0:T(8,128)(2,1)S(1)}) custom-call(bf16[32,2048]{1,0:T(8,128)(2,1)S(1)} %collective-permute-done.6.refs_0_, bf16[80,2048]{1,0:T(8,128)(2,1)S(1)} %collective-permute-done.7.refs_1_, bf16[1,2048]{1,0:T(2,128)(2,1)S(1)} %copy-done.1, bf16[8,2048]{1,0:T(8,128)(2,1)S(1)} %bitcast.21, ...), custom_call_target="tpu_custom_call" | custom-call | flops 1 | bytes 1 | tf_op jit(solution)/shard_map/experts/pallas_call | solution.py:247
  37.7 0.1 collective-permute-start.13
  37.8 5.2 %collective-permute-start.8 = (bf16[32,2048]{1,0:T(8,128)(2,1)S(1)}, bf16[32,2048]{1,0:T(8,128)(2,1)S(1)}, u32[]{:S(2)}, u32[]{:S(2)}) collective-permute-start(bf16[32,2048]{1,0:T(8,128)(2,1)S(1)} %get-tuple-element.37.refs_7_), channel_id=1, source_target_pairs={{0,28},{1,29},{2,30},{3,31},{4,24},{5,25},{6,26},{7,27},{8,4},{9,5... | collective-permute-start | bytes 393224 | tf_op jit(solution)/shard_map/ppermute | solution.py:22
  43.0 1.9 %collective-permute-done.10.refs_1_ = bf16[48,2048]{1,0:T(8,128)(2,1)S(1)} collective-permute-done((bf16[48,2048]{1,0:T(8,128)(2,1)S(1)}, bf16[48,2048]{1,0:T(8,128)(2,1)S(1)}, u32[]{:S(2)}, u32[]{:S(2)}) %collective-permute-start.10) | collective-permute-done | bytes 196640 | tf_op jit(solution)/shard_map/ppermute | solution.py:22
  44.8 2.3 %experts.5 = (bf16[48,2048]{1,0:T(8,128)(2,1)S(1)}, bf16[48,2048]{1,0:T(8,128)(2,1)S(1)}) custom-call(bf16[48,2048]{1,0:T(8,128)(2,1)S(1)} %collective-permute-done.9.refs_0_, bf16[48,2048]{1,0:T(8,128)(2,1)S(1)} %collective-permute-done.10.refs_1_, bf16[1,2048]{1,0:T(2,128)(2,1)S(1)} %copy-done.1, bf16[8,2048]{1,0:T(8,128)(2,1)S(1)} %bitcast.22, ...), custom_call_target="tpu_custom_call" | custom-call | flops 1 | bytes 1 | tf_op jit(solution)/shard_map/experts/pallas_call | solution.py:247
  47.1 1.3 %collective-permute-start.11 = (bf16[48,2048]{1,0:T(8,128)(2,1)S(1)}, bf16[48,2048]{1,0:T(8,128)(2,1)S(1)}, u32[]{:S(2)}, u32[]{:S(2)}) collective-permute-start(bf16[48,2048]{1,0:T(8,128)(2,1)S(1)} %get-tuple-element.40), channel_id=1, source_target_pairs={{0,30},{1,31},{2,28},{3,29},{4,26},{5,27},{6,24},{7,25},{8,6},{9,7... | collective-permute-start | bytes 589832 | tf_op jit(solution)/shard_map/ppermute | solution.py:22
  48.5 16.2 %collective-permute-start.5 = (bf16[32,2048]{1,0:T(8,128)(2,1)S(1)}, bf16[32,2048]{1,0:T(8,128)(2,1)S(1)}, u32[]{:S(2)}, u32[]{:S(2)}) collective-permute-start(bf16[32,2048]{1,0:T(8,128)(2,1)S(1)} %get-tuple-element.34.refs_7_), channel_id=1, source_target_pairs={{0,30},{1,31},{2,28},{3,29},{4,26},{5,27},{6,24},{7,25},{8,6},{9,7... | collective-permute-start | bytes 393224 | tf_op jit(solution)/shard_map/ppermute | solution.py:22
  64.6 2.5 %collective-permute-done.5.refs_0_ = bf16[32,2048]{1,0:T(8,128)(2,1)S(1)} collective-permute-done((bf16[32,2048]{1,0:T(8,128)(2,1)S(1)}, bf16[32,2048]{1,0:T(8,128)(2,1)S(1)}, u32[]{:S(2)}, u32[]{:S(2)}) %collective-permute-start.5) | collective-permute-done | bytes 131104 | tf_op jit(solution)/shard_map/ppermute | solution.py:22
  67.2 3.4 %collective-permute-done.12.refs_3_ = bf16[48,2048]{1,0:T(8,128)(2,1)S(1)} collective-permute-done((bf16[48,2048]{1,0:T(8,128)(2,1)S(1)}, bf16[48,2048]{1,0:T(8,128)(2,1)S(1)}, u32[]{:S(2)}, u32[]{:S(2)}) %collective-permute-start.12) | collective-permute-done | bytes 196640 | tf_op jit(solution)/shard_map/ppermute | solution.py:22
  70.6 0.1 collective-permute-start.14
  70.8 0.5 collective-permute-start.15
  71.4 0.5 weights.1
  71.9 0.1 copy.8
  72.0 0.1 copy.9
  72.2 0.4 combine.1.base_ref
  72.6 0.1 slice_bitcast_fusion
  72.7 0.1 collective-permute-done.15.refs_2_
  72.8 1.1 %finish.1 = bf16[128,2048]{1,0:T(8,128)(2,1)} custom-call(f32[128,2048]{1,0:T(8,128)S(1)} %combine.1.base_ref, bf16[128,200]{1,0:T(8,128)(2,1)S(1)} %get-tuple-element.46.high_ref, bf16[128,200]{1,0:T(8,128)(2,1)S(1)} %get-tuple-element.45.low_ref, bf16[40,2048]{1,0:T(8,128)(2,1)S(1)} %slice.54.refs_0_, ...), custom_call_target="tpu_custom_call" | custom-call | flops 1 | bytes 1 | tf_op jit(solution)/shard_map/finish/pallas_call | solution.py:216
  (26 shorter events, 0.2 us)
Async XLA Ops:
  0.0 2.2 %collective-permute-start.1 = (bf16[128,2048]{1,0:T(8,128)(2,1)}, bf16[128,2048]{1,0:T(8,128)(2,1)S(1)}, u32[]{:S(2)}, u32[]{:S(2)}) collective-permute-start(bf16[128,2048]{1,0:T(8,128)(2,1)} %bitcast.26), channel_id=1, source_target_pairs={{0,1},{1,0},{2,3},{3,2},{4,5},{5,4},{6,7},{7,6},{8,9},{9,8},{10,11... | collective-permute-start | bytes 1572872 | tf_op jit(solution)/shard_map/ppermute | solution.py:22
  0.5 1.8 %collective-permute-start = (s32[2,2,64]{2,1,0:T(2,128)}, s32[2,2,64]{2,1,0:T(2,128)S(1)}, u32[]{:S(2)}, u32[]{:S(2)}) collective-permute-start(s32[2,2,64]{2,1,0:T(2,128)} %bitcast.28), channel_id=1, source_target_pairs={{0,1},{1,0},{2,3},{3,2},{4,5},{5,4},{6,7},{7,6},{8,9},{9,8},{10,11... | collective-permute-start | bytes 3080 | tf_op jit(solution)/shard_map/ppermute | solution.py:22
  3.0 25.3 %collective-permute-start.3 = (bf16[80,2048]{1,0:T(8,128)(2,1)S(1)}, bf16[80,2048]{1,0:T(8,128)(2,1)S(1)}, u32[]{:S(2)}, u32[]{:S(2)}) collective-permute-start(bf16[80,2048]{1,0:T(8,128)(2,1)S(1)} %get-tuple-element.27), channel_id=1, source_target_pairs={{0,8},{1,9},{2,10},{3,11},{4,12},{5,13},{6,14},{7,15},{8,16},{9,17... | collective-permute-start | bytes 983048 | tf_op jit(solution)/shard_map/ppermute | solution.py:22
  5.9 29.7 %collective-permute-start.7 = (bf16[80,2048]{1,0:T(8,128)(2,1)S(1)}, bf16[80,2048]{1,0:T(8,128)(2,1)S(1)}, u32[]{:S(2)}, u32[]{:S(2)}) collective-permute-start(bf16[80,2048]{1,0:T(8,128)(2,1)S(1)} %get-tuple-element.36), channel_id=1, source_target_pairs={{0,10},{1,11},{2,8},{3,9},{4,14},{5,15},{6,12},{7,13},{8,18},{9,19... | collective-permute-start | bytes 983048 | tf_op jit(solution)/shard_map/ppermute | solution.py:22
  8.4 17.6 %collective-permute-start.2 = (bf16[32,2048]{1,0:T(8,128)(2,1)S(1)}, bf16[32,2048]{1,0:T(8,128)(2,1)S(1)}, u32[]{:S(2)}, u32[]{:S(2)}) collective-permute-start(bf16[32,2048]{1,0:T(8,128)(2,1)S(1)} %get-tuple-element.26), channel_id=1, source_target_pairs={{0,14},{1,15},{2,12},{3,13},{4,10},{5,11},{6,8},{7,9},{8,22},{9,23... | collective-permute-start | bytes 393224 | tf_op jit(solution)/shard_map/ppermute | solution.py:22
  11.8 23.8 %collective-permute-start.6 = (bf16[32,2048]{1,0:T(8,128)(2,1)S(1)}, bf16[32,2048]{1,0:T(8,128)(2,1)S(1)}, u32[]{:S(2)}, u32[]{:S(2)}) collective-permute-start(bf16[32,2048]{1,0:T(8,128)(2,1)S(1)} %get-tuple-element.35), channel_id=1, source_target_pairs={{0,12},{1,13},{2,14},{3,15},{4,8},{5,9},{6,10},{7,11},{8,20},{9,21... | collective-permute-start | bytes 393224 | tf_op jit(solution)/shard_map/ppermute | solution.py:22
  11.9 16.4 %copy-start = (bf16[1,2048,8]{1,2,0:T(8,128)(2,1)S(1)}, bf16[1,2048,8]{1,2,0:T(8,128)(2,1)}, u32[]{:S(2)}) copy-start(bf16[1,2048,8]{1,2,0:T(8,128)(2,1)} %param.10) | copy-start | bytes 98308
  11.9 16.4 %copy-start.1 = (bf16[1,2048]{1,0:T(2,128)(2,1)S(1)}, bf16[1,2048]{1,0:T(2,128)(2,1)}, u32[]{:S(2)}) copy-start(bf16[1,2048]{1,0:T(2,128)(2,1)} %refs_2_.5) | copy-start | bytes 12292
  16.6 26.3 %collective-permute-start.9 = (bf16[48,2048]{1,0:T(8,128)(2,1)S(1)}, bf16[48,2048]{1,0:T(8,128)(2,1)S(1)}, u32[]{:S(2)}, u32[]{:S(2)}) collective-permute-start(bf16[48,2048]{1,0:T(8,128)(2,1)S(1)} %get-tuple-element.38), channel_id=1, source_target_pairs={{0,14},{1,15},{2,12},{3,13},{4,10},{5,11},{6,8},{7,9},{8,22},{9,23... | collective-permute-start | bytes 589832 | tf_op jit(solution)/shard_map/ppermute | solution.py:22
  26.1 18.8 %collective-permute-start.10 = (bf16[48,2048]{1,0:T(8,128)(2,1)S(1)}, bf16[48,2048]{1,0:T(8,128)(2,1)S(1)}, u32[]{:S(2)}, u32[]{:S(2)}) collective-permute-start(bf16[48,2048]{1,0:T(8,128)(2,1)S(1)} %get-tuple-element.39), channel_id=1, source_target_pairs={{0,12},{1,13},{2,14},{3,15},{4,8},{5,9},{6,10},{7,11},{8,20},{9,21... | collective-permute-start | bytes 589832 | tf_op jit(solution)/shard_map/ppermute | solution.py:22
  30.5 40.1 %collective-permute-start.4 = (bf16[96,2048]{1,0:T(8,128)(2,1)S(1)}, bf16[96,2048]{1,0:T(8,128)(2,1)S(1)}, u32[]{:S(2)}, u32[]{:S(2)}) collective-permute-start(bf16[96,2048]{1,0:T(8,128)(2,1)S(1)} %get-tuple-element.31), channel_id=1, source_target_pairs={{0,24},{1,25},{2,26},{3,27},{4,28},{5,29},{6,30},{7,31},{8,0},{9,1... | collective-permute-start | bytes 1179656 | tf_op jit(solution)/shard_map/ppermute | solution.py:22
  37.7 33.0 %collective-permute-start.13 = (bf16[80,2048]{1,0:T(8,128)(2,1)S(1)}, bf16[80,2048]{1,0:T(8,128)(2,1)S(1)}, u32[]{:S(2)}, u32[]{:S(2)}) collective-permute-start(bf16[80,2048]{1,0:T(8,128)(2,1)S(1)} %get-tuple-element.42), channel_id=1, source_target_pairs={{0,26},{1,27},{2,24},{3,25},{4,30},{5,31},{6,28},{7,29},{8,2},{9,3... | collective-permute-start | bytes 983048 | tf_op jit(solution)/shard_map/ppermute | solution.py:22
  37.8 10.6 %collective-permute-start.8 = (bf16[32,2048]{1,0:T(8,128)(2,1)S(1)}, bf16[32,2048]{1,0:T(8,128)(2,1)S(1)}, u32[]{:S(2)}, u32[]{:S(2)}) collective-permute-start(bf16[32,2048]{1,0:T(8,128)(2,1)S(1)} %get-tuple-element.37.refs_7_), channel_id=1, source_target_pairs={{0,28},{1,29},{2,30},{3,31},{4,24},{5,25},{6,26},{7,27},{8,4},{9,5... | collective-permute-start | bytes 393224 | tf_op jit(solution)/shard_map/ppermute | solution.py:22
  47.1 20.0 %collective-permute-start.11 = (bf16[48,2048]{1,0:T(8,128)(2,1)S(1)}, bf16[48,2048]{1,0:T(8,128)(2,1)S(1)}, u32[]{:S(2)}, u32[]{:S(2)}) collective-permute-start(bf16[48,2048]{1,0:T(8,128)(2,1)S(1)} %get-tuple-element.40), channel_id=1, source_target_pairs={{0,30},{1,31},{2,28},{3,29},{4,26},{5,27},{6,24},{7,25},{8,6},{9,7... | collective-permute-start | bytes 589832 | tf_op jit(solution)/shard_map/ppermute | solution.py:22
  48.5 22.1 %collective-permute-start.12 = (bf16[48,2048]{1,0:T(8,128)(2,1)S(1)}, bf16[48,2048]{1,0:T(8,128)(2,1)S(1)}, u32[]{:S(2)}, u32[]{:S(2)}) collective-permute-start(bf16[48,2048]{1,0:T(8,128)(2,1)S(1)} %get-tuple-element.41), channel_id=1, source_target_pairs={{0,28},{1,29},{2,30},{3,31},{4,24},{5,25},{6,26},{7,27},{8,4},{9,5... | collective-permute-start | bytes 589832 | tf_op jit(solution)/shard_map/ppermute | solution.py:22
  48.5 18.7 %collective-permute-start.5 = (bf16[32,2048]{1,0:T(8,128)(2,1)S(1)}, bf16[32,2048]{1,0:T(8,128)(2,1)S(1)}, u32[]{:S(2)}, u32[]{:S(2)}) collective-permute-start(bf16[32,2048]{1,0:T(8,128)(2,1)S(1)} %get-tuple-element.34.refs_7_), channel_id=1, source_target_pairs={{0,30},{1,31},{2,28},{3,29},{4,26},{5,27},{6,24},{7,25},{8,6},{9,7... | collective-permute-start | bytes 393224 | tf_op jit(solution)/shard_map/ppermute | solution.py:22
  70.6 2.2 %collective-permute-start.14 = (bf16[120,2048]{1,0:T(8,128)(2,1)S(1)}, bf16[120,2048]{1,0:T(8,128)(2,1)S(1)}, u32[]{:S(2)}, u32[]{:S(2)}) collective-permute-start(bf16[120,2048]{1,0:T(8,128)(2,1)S(1)} %stack.2), channel_id=1, source_target_pairs={{0,1},{1,0},{2,3},{3,2},{4,5},{5,4},{6,7},{7,6},{8,9},{9,8},{10,11... | collective-permute-start | bytes 1474568 | tf_op jit(solution)/shard_map/ppermute | solution.py:22
  70.8 2.0 %collective-permute-start.15 = (bf16[40,2048]{1,0:T(8,128)(2,1)S(1)}, bf16[40,2048]{1,0:T(8,128)(2,1)S(1)}, u32[]{:S(2)}, u32[]{:S(2)}) collective-permute-start(bf16[40,2048]{1,0:T(8,128)(2,1)S(1)} %stack.3), channel_id=1, source_target_pairs={{0,1},{1,0},{2,3},{3,2},{4,5},{5,4},{6,7},{7,6},{8,9},{9,8},{10,11... | collective-permute-start | bytes 491528 | tf_op jit(solution)/shard_map/ppermute | solution.py:22

commit v5 on v4

--- a/solution.py
+++ b/solution.py
@@ -159,7 +159,7 @@
     blocks, (out_ref, done_ref, sems) = refs[:-3], refs[-3:]
     high, low = high_ref[...], low_ref[...]
     copies = []
-    for at, span in enumerate(tiles(base_ref.shape[1], min(512, base_ref.shape[1]))):
+    for at, span in enumerate(tiles(base_ref.shape[1], min(1024, base_ref.shape[1]))):
         values = jnp.concatenate([ref[:, span] for ref in blocks], axis=0)
         total = base_ref[:, span]
         total += jnp.dot(high, values, preferred_element_type=jnp.float32)
@@ -220,7 +220,7 @@
         out_shape=jax.ShapeDtypeStruct((rows, features), jnp.bfloat16),
         scratch_shapes=[
             pltpu.VMEM((rows, features), jnp.bfloat16),
-            pltpu.SemaphoreType.DMA((len(tiles(features, min(512, features))),)),
+            pltpu.SemaphoreType.DMA((len(tiles(features, min(1024, features))),)),
         ],
         compiler_params=PARAMS,
         cost_estimate=CHEAP,
@@ -266,6 +266,7 @@
 TEAMS = ((0, 3), (1, 2), (4, 5))
 BACK = (0, 1, 4, 5, 2, 3)
 RIDER = 3
+PACKS = ((2, 3, 0), (1, 4, 5))
 SWAPS = ((0, 1, 4, 5, 3), (2,))
 
 
@@ -289,15 +290,21 @@
 
     other_rows, other_chosen = moved(rows, 0, 1), moved(chosen, 0, 1)
     held_rows, held_chosen = load(rows, chosen)
-    outgoing = pl.pallas_call(
-        functools.partial(pack_kernel, width, groups, flows),
-        in_specs=[SMEM] + [VMEM] * 4,
-        out_specs=[VMEM] * len(flows),
-        out_shape=[jax.ShapeDtypeStruct((rows_of, features), jnp.bfloat16) for rows_of in sizes],
-        compiler_params=PARAMS,
-        cost_estimate=CHEAP,
-        name="pack",
-    )(me, held_chosen, other_chosen, held_rows, other_rows)
+    def pack(part):
+        return pl.pallas_call(
+            functools.partial(pack_kernel, width, groups, [flows[f] for f in part]),
+            in_specs=[SMEM] + [VMEM] * 4,
+            out_specs=[VMEM] * len(part),
+            out_shape=[jax.ShapeDtypeStruct((sizes[f], features), jnp.bfloat16) for f in part],
+            compiler_params=PARAMS,
+            cost_estimate=CHEAP,
+            name="pack",
+        )(me, held_chosen, other_chosen, held_rows, other_rows)
+
+    outgoing = [None] * len(flows)
+    for part in (pick(PACKS[0]), pick(PACKS[1])):
+        for f, block in zip(part, pack(part)):
+            outgoing[f] = block
     arrived = [moved(block, 1, flow[0]) for block, flow in zip(outgoing, flows)]
 
     held = load(gate_weight[0], up_weight[0], down_weight[0])

time: 74.1 us -> 74.2 us (level)
  starting transfers between devices: 41.6 us -> 30.9 us
  waiting for transfers between devices: 16.5 us -> 26.7 us
    ppermute x16, starting transfers between devices: 41.6 us -> 30.9 us  [moved(): return lax.ppermute(block, HOME, pairs)]
    ppermute x16, waiting for transfers between devices: 16.5 us -> 26.7 us  [moved(): return lax.ppermute(block, HOME, pairs)]
  transfers between devices with their start and end apart: 16 -> 16, of which waited for: 7 -> 8; matrix products, arithmetic and copies ran while one was open for 1% -> 1% of each run, Pallas kernels for 18% -> 19%
where the time goes in v5:
time: 74.2 us; the launch traced here: 74 us
  starting transfers between devices  30.9 us (42%)
  waiting for transfers between devices  26.7 us (36%)
  Pallas kernels  15.8 us (21%)
    ppermute x16, starting transfers between devices, moved(): return lax.ppermute(block, HOME, pairs)  30.9 us
    ppermute x16, waiting for transfers between devices, moved(): return lax.ppermute(block, HOME, pairs)  26.7 us
    pallas_call x3, Pallas kernels, run_experts(): pl.pallas_call(functools.partial(expert_kernel, tuple(sizes), ride), in_s...  6.64 us
    pallas_call x2, Pallas kernels, load(): pl.pallas_call(functools.partial(load_kernel, len(arrays)), in_specs=[HBM...  5.75 us
  transfers between devices with their start and end apart: 16, of which 8 were waited for; matrix products, arithmetic and copies ran while one was open for 1% of the time, Pallas kernels for 19%

profile of v5, /device:TPU:0, one launch (start us, length us, event | category | flops | bytes accessed | tf_op | source)
XLA Modules:
  0.0 74.0 jit_solution(6729082077529040127)
XLA Ops:
  0.0 0.5 collective-permute-start.1
  0.5 1.1 %load.2 = (bf16[128,2048]{1,0:T(8,128)(2,1)S(1)}, s32[2,2,64]{2,1,0:T(2,128)S(1)}) custom-call(bf16[128,2048]{1,0:T(8,128)(2,1)} %bitcast.27, s32[2,2,64]{2,1,0:T(2,128)} %bitcast.29), custom_call_target="tpu_custom_call" | custom-call | flops 1 | bytes 1 | tf_op jit(solution)/shard_map/load/pallas_call | solution.py:190
  1.6 0.6 collective-permute-done.refs_1_
  2.2 0.7 pack.2
  2.9 2.9 %collective-permute-start.3 = (bf16[80,2048]{1,0:T(8,128)(2,1)S(1)}, bf16[80,2048]{1,0:T(8,128)(2,1)S(1)}, u32[]{:S(2)}, u32[]{:S(2)}) collective-permute-start(bf16[80,2048]{1,0:T(8,128)(2,1)S(1)} %get-tuple-element.27), channel_id=1, source_target_pairs={{0,8},{1,9},{2,10},{3,11},{4,12},{5,13},{6,14},{7,15},{8,16},{9,17... | collective-permute-start | bytes 983048 | tf_op jit(solution)/shard_map/ppermute | solution.py:22
  5.8 2.5 %collective-permute-start.7 = (bf16[80,2048]{1,0:T(8,128)(2,1)S(1)}, bf16[80,2048]{1,0:T(8,128)(2,1)S(1)}, u32[]{:S(2)}, u32[]{:S(2)}) collective-permute-start(bf16[80,2048]{1,0:T(8,128)(2,1)S(1)} %get-tuple-element.36), channel_id=1, source_target_pairs={{0,10},{1,11},{2,8},{3,9},{4,14},{5,15},{6,12},{7,13},{8,18},{9,19... | collective-permute-start | bytes 983048 | tf_op jit(solution)/shard_map/ppermute | solution.py:22
  8.3 3.4 %collective-permute-start.2 = (bf16[32,2048]{1,0:T(8,128)(2,1)S(1)}, bf16[32,2048]{1,0:T(8,128)(2,1)S(1)}, u32[]{:S(2)}, u32[]{:S(2)}) collective-permute-start(bf16[32,2048]{1,0:T(8,128)(2,1)S(1)} %get-tuple-element.26), channel_id=1, source_target_pairs={{0,14},{1,15},{2,12},{3,13},{4,10},{5,11},{6,8},{7,9},{8,22},{9,23... | collective-permute-start | bytes 393224 | tf_op jit(solution)/shard_map/ppermute | solution.py:22
  11.7 0.6 pack.3
  12.3 0.2 collective-permute-start.6
  12.5 4.7 %load.3 = (bf16[2048,1024]{1,0:T(8,128)(2,1)S(1)}, bf16[2048,1024]{1,0:T(8,128)(2,1)S(1)}, bf16[1024,2048]{1,0:T(8,128)(2,1)S(1)}) custom-call(bf16[2048,1024]{1,0:T(8,128)(2,1)} %bitcast.23, bf16[2048,1024]{1,0:T(8,128)(2,1)} %bitcast.24, bf16[1024,2048]{1,0:T(8,128)(2,1)} %bitcast.25), custom_call_target="tpu_custom_call" | custom-call | flops 1 | bytes 1 | tf_op jit(solution)/shard_map/load/pallas_call | solution.py:190
  17.2 3.8 %collective-permute-start.9 = (bf16[48,2048]{1,0:T(8,128)(2,1)S(1)}, bf16[48,2048]{1,0:T(8,128)(2,1)S(1)}, u32[]{:S(2)}, u32[]{:S(2)}) collective-permute-start(bf16[48,2048]{1,0:T(8,128)(2,1)S(1)} %get-tuple-element.38), channel_id=1, source_target_pairs={{0,14},{1,15},{2,12},{3,13},{4,10},{5,11},{6,8},{7,9},{8,22},{9,23... | collective-permute-start | bytes 589832 | tf_op jit(solution)/shard_map/ppermute | solution.py:22
  21.0 4.9 %collective-permute-done.2.refs_0_ = bf16[32,2048]{1,0:T(8,128)(2,1)S(1)} collective-permute-done((bf16[32,2048]{1,0:T(8,128)(2,1)S(1)}, bf16[32,2048]{1,0:T(8,128)(2,1)S(1)}, u32[]{:S(2)}, u32[]{:S(2)}) %collective-permute-start.2) | collective-permute-done | bytes 131104 | tf_op jit(solution)/shard_map/ppermute | solution.py:22
  25.9 2.3 %collective-permute-done.3.refs_1_ = bf16[80,2048]{1,0:T(8,128)(2,1)S(1)} collective-permute-done((bf16[80,2048]{1,0:T(8,128)(2,1)S(1)}, bf16[80,2048]{1,0:T(8,128)(2,1)S(1)}, u32[]{:S(2)}, u32[]{:S(2)}) %collective-permute-start.3) | collective-permute-done | bytes 327712 | tf_op jit(solution)/shard_map/ppermute | solution.py:22
  28.2 2.2 %experts.3 = (bf16[32,2048]{1,0:T(8,128)(2,1)S(1)}, bf16[96,2048]{1,0:T(8,128)(2,1)S(1)}) custom-call(bf16[32,2048]{1,0:T(8,128)(2,1)S(1)} %collective-permute-done.2.refs_0_, bf16[80,2048]{1,0:T(8,128)(2,1)S(1)} %collective-permute-done.3.refs_1_, bf16[1,2048]{1,0:T(2,128)(2,1)S(1)} %copy-done.1, bf16[8,2048]{1,0:T(8,128)(2,1)S(1)} %bitcast.20, ...), custom_call_target="tpu_custom_call" | custom-call | flops 1 | bytes 1 | tf_op jit(solution)/shard_map/experts/pallas_call | solution.py:247
  30.4 5.1 %collective-permute-start.4 = (bf16[96,2048]{1,0:T(8,128)(2,1)S(1)}, bf16[96,2048]{1,0:T(8,128)(2,1)S(1)}, u32[]{:S(2)}, u32[]{:S(2)}) collective-permute-start(bf16[96,2048]{1,0:T(8,128)(2,1)S(1)} %get-tuple-element.31), channel_id=1, source_target_pairs={{0,24},{1,25},{2,26},{3,27},{4,28},{5,29},{6,30},{7,31},{8,0},{9,1... | collective-permute-start | bytes 1179656 | tf_op jit(solution)/shard_map/ppermute | solution.py:22
  35.5 2.2 %experts.4 = (bf16[32,2048]{1,0:T(8,128)(2,1)S(1)}, bf16[80,2048]{1,0:T(8,128)(2,1)S(1)}) custom-call(bf16[32,2048]{1,0:T(8,128)(2,1)S(1)} %collective-permute-done.6.refs_0_, bf16[80,2048]{1,0:T(8,128)(2,1)S(1)} %collective-permute-done.7.refs_1_, bf16[1,2048]{1,0:T(2,128)(2,1)S(1)} %copy-done.1, bf16[8,2048]{1,0:T(8,128)(2,1)S(1)} %bitcast.21, ...), custom_call_target="tpu_custom_call" | custom-call | flops 1 | bytes 1 | tf_op jit(solution)/shard_map/experts/pallas_call | solution.py:247
  37.7 5.1 %collective-permute-start.8 = (bf16[32,2048]{1,0:T(8,128)(2,1)S(1)}, bf16[32,2048]{1,0:T(8,128)(2,1)S(1)}, u32[]{:S(2)}, u32[]{:S(2)}) collective-permute-start(bf16[32,2048]{1,0:T(8,128)(2,1)S(1)} %get-tuple-element.37.refs_7_), channel_id=1, source_target_pairs={{0,28},{1,29},{2,30},{3,31},{4,24},{5,25},{6,26},{7,27},{8,4},{9,5... | collective-permute-start | bytes 393224 | tf_op jit(solution)/shard_map/ppermute | solution.py:22
  42.8 1.9 %collective-permute-done.10.refs_1_ = bf16[48,2048]{1,0:T(8,128)(2,1)S(1)} collective-permute-done((bf16[48,2048]{1,0:T(8,128)(2,1)S(1)}, bf16[48,2048]{1,0:T(8,128)(2,1)S(1)}, u32[]{:S(2)}, u32[]{:S(2)}) %collective-permute-start.10) | collective-permute-done | bytes 196640 | tf_op jit(solution)/shard_map/ppermute | solution.py:22
  44.8 2.3 %experts.5 = (bf16[48,2048]{1,0:T(8,128)(2,1)S(1)}, bf16[48,2048]{1,0:T(8,128)(2,1)S(1)}) custom-call(bf16[48,2048]{1,0:T(8,128)(2,1)S(1)} %collective-permute-done.9.refs_0_, bf16[48,2048]{1,0:T(8,128)(2,1)S(1)} %collective-permute-done.10.refs_1_, bf16[1,2048]{1,0:T(2,128)(2,1)S(1)} %copy-done.1, bf16[8,2048]{1,0:T(8,128)(2,1)S(1)} %bitcast.22, ...), custom_call_target="tpu_custom_call" | custom-call | flops 1 | bytes 1 | tf_op jit(solution)/shard_map/experts/pallas_call | solution.py:247
  47.1 1.2 %collective-permute-start.11 = (bf16[48,2048]{1,0:T(8,128)(2,1)S(1)}, bf16[48,2048]{1,0:T(8,128)(2,1)S(1)}, u32[]{:S(2)}, u32[]{:S(2)}) collective-permute-start(bf16[48,2048]{1,0:T(8,128)(2,1)S(1)} %get-tuple-element.40), channel_id=1, source_target_pairs={{0,30},{1,31},{2,28},{3,29},{4,26},{5,27},{6,24},{7,25},{8,6},{9,7... | collective-permute-start | bytes 589832 | tf_op jit(solution)/shard_map/ppermute | solution.py:22
  48.3 0.2 collective-permute-done.8.refs_1_
  48.6 5.5 %collective-permute-start.5 = (bf16[32,2048]{1,0:T(8,128)(2,1)S(1)}, bf16[32,2048]{1,0:T(8,128)(2,1)S(1)}, u32[]{:S(2)}, u32[]{:S(2)}) collective-permute-start(bf16[32,2048]{1,0:T(8,128)(2,1)S(1)} %get-tuple-element.34.refs_7_), channel_id=1, source_target_pairs={{0,30},{1,31},{2,28},{3,29},{4,26},{5,27},{6,24},{7,25},{8,6},{9,7... | collective-permute-start | bytes 393224 | tf_op jit(solution)/shard_map/ppermute | solution.py:22
  54.1 8.3 %collective-permute-done.5.refs_0_ = bf16[32,2048]{1,0:T(8,128)(2,1)S(1)} collective-permute-done((bf16[32,2048]{1,0:T(8,128)(2,1)S(1)}, bf16[32,2048]{1,0:T(8,128)(2,1)S(1)}, u32[]{:S(2)}, u32[]{:S(2)}) %collective-permute-start.5) | collective-permute-done | bytes 131104 | tf_op jit(solution)/shard_map/ppermute | solution.py:22
  62.4 8.2 %collective-permute-done.12.refs_3_ = bf16[48,2048]{1,0:T(8,128)(2,1)S(1)} collective-permute-done((bf16[48,2048]{1,0:T(8,128)(2,1)S(1)}, bf16[48,2048]{1,0:T(8,128)(2,1)S(1)}, u32[]{:S(2)}, u32[]{:S(2)}) %collective-permute-start.12) | collective-permute-done | bytes 196640 | tf_op jit(solution)/shard_map/ppermute | solution.py:22
  70.8 0.5 collective-permute-start.15
  71.4 0.5 weights.1
  71.9 0.1 copy.8
  72.0 0.1 copy.9
  72.2 0.4 combine.1.base_ref
  72.6 0.1 slice_bitcast_fusion
  72.7 0.1 collective-permute-done.15.refs_2_
  72.8 1.2 %finish.1 = bf16[128,2048]{1,0:T(8,128)(2,1)} custom-call(f32[128,2048]{1,0:T(8,128)S(1)} %combine.1.base_ref, bf16[128,200]{1,0:T(8,128)(2,1)S(1)} %get-tuple-element.46.high_ref, bf16[128,200]{1,0:T(8,128)(2,1)S(1)} %get-tuple-element.45.low_ref, bf16[40,2048]{1,0:T(8,128)(2,1)S(1)} %slice.54.refs_0_, ...), custom_call_target="tpu_custom_call" | custom-call | flops 1 | bytes 1 | tf_op jit(solution)/shard_map/finish/pallas_call | solution.py:216
  (27 shorter events, 0.3 us)
Async XLA Ops:
  0.0 2.2 %collective-permute-start.1 = (bf16[128,2048]{1,0:T(8,128)(2,1)}, bf16[128,2048]{1,0:T(8,128)(2,1)S(1)}, u32[]{:S(2)}, u32[]{:S(2)}) collective-permute-start(bf16[128,2048]{1,0:T(8,128)(2,1)} %bitcast.26), channel_id=1, source_target_pairs={{0,1},{1,0},{2,3},{3,2},{4,5},{5,4},{6,7},{7,6},{8,9},{9,8},{10,11... | collective-permute-start | bytes 1572872 | tf_op jit(solution)/shard_map/ppermute | solution.py:22
  0.5 1.8 %collective-permute-start = (s32[2,2,64]{2,1,0:T(2,128)}, s32[2,2,64]{2,1,0:T(2,128)S(1)}, u32[]{:S(2)}, u32[]{:S(2)}) collective-permute-start(s32[2,2,64]{2,1,0:T(2,128)} %bitcast.28), channel_id=1, source_target_pairs={{0,1},{1,0},{2,3},{3,2},{4,5},{5,4},{6,7},{7,6},{8,9},{9,8},{10,11... | collective-permute-start | bytes 3080 | tf_op jit(solution)/shard_map/ppermute | solution.py:22
  2.9 25.3 %collective-permute-start.3 = (bf16[80,2048]{1,0:T(8,128)(2,1)S(1)}, bf16[80,2048]{1,0:T(8,128)(2,1)S(1)}, u32[]{:S(2)}, u32[]{:S(2)}) collective-permute-start(bf16[80,2048]{1,0:T(8,128)(2,1)S(1)} %get-tuple-element.27), channel_id=1, source_target_pairs={{0,8},{1,9},{2,10},{3,11},{4,12},{5,13},{6,14},{7,15},{8,16},{9,17... | collective-permute-start | bytes 983048 | tf_op jit(solution)/shard_map/ppermute | solution.py:22
  5.8 29.7 %collective-permute-start.7 = (bf16[80,2048]{1,0:T(8,128)(2,1)S(1)}, bf16[80,2048]{1,0:T(8,128)(2,1)S(1)}, u32[]{:S(2)}, u32[]{:S(2)}) collective-permute-start(bf16[80,2048]{1,0:T(8,128)(2,1)S(1)} %get-tuple-element.36), channel_id=1, source_target_pairs={{0,10},{1,11},{2,8},{3,9},{4,14},{5,15},{6,12},{7,13},{8,18},{9,19... | collective-permute-start | bytes 983048 | tf_op jit(solution)/shard_map/ppermute | solution.py:22
  8.3 17.6 %collective-permute-start.2 = (bf16[32,2048]{1,0:T(8,128)(2,1)S(1)}, bf16[32,2048]{1,0:T(8,128)(2,1)S(1)}, u32[]{:S(2)}, u32[]{:S(2)}) collective-permute-start(bf16[32,2048]{1,0:T(8,128)(2,1)S(1)} %get-tuple-element.26), channel_id=1, source_target_pairs={{0,14},{1,15},{2,12},{3,13},{4,10},{5,11},{6,8},{7,9},{8,22},{9,23... | collective-permute-start | bytes 393224 | tf_op jit(solution)/shard_map/ppermute | solution.py:22
  12.3 23.2 %collective-permute-start.6 = (bf16[32,2048]{1,0:T(8,128)(2,1)S(1)}, bf16[32,2048]{1,0:T(8,128)(2,1)S(1)}, u32[]{:S(2)}, u32[]{:S(2)}) collective-permute-start(bf16[32,2048]{1,0:T(8,128)(2,1)S(1)} %get-tuple-element.35), channel_id=1, source_target_pairs={{0,12},{1,13},{2,14},{3,15},{4,8},{5,9},{6,10},{7,11},{8,20},{9,21... | collective-permute-start | bytes 393224 | tf_op jit(solution)/shard_map/ppermute | solution.py:22
  12.5 15.7 %copy-start = (bf16[1,2048,8]{1,2,0:T(8,128)(2,1)S(1)}, bf16[1,2048,8]{1,2,0:T(8,128)(2,1)}, u32[]{:S(2)}) copy-start(bf16[1,2048,8]{1,2,0:T(8,128)(2,1)} %param.10) | copy-start | bytes 98308
  12.5 15.7 %copy-start.1 = (bf16[1,2048]{1,0:T(2,128)(2,1)S(1)}, bf16[1,2048]{1,0:T(2,128)(2,1)}, u32[]{:S(2)}) copy-start(bf16[1,2048]{1,0:T(2,128)(2,1)} %refs_2_.5) | copy-start | bytes 12292
  17.2 25.7 %collective-permute-start.9 = (bf16[48,2048]{1,0:T(8,128)(2,1)S(1)}, bf16[48,2048]{1,0:T(8,128)(2,1)S(1)}, u32[]{:S(2)}, u32[]{:S(2)}) collective-permute-start(bf16[48,2048]{1,0:T(8,128)(2,1)S(1)} %get-tuple-element.38), channel_id=1, source_target_pairs={{0,14},{1,15},{2,12},{3,13},{4,10},{5,11},{6,8},{7,9},{8,22},{9,23... | collective-permute-start | bytes 589832 | tf_op jit(solution)/shard_map/ppermute | solution.py:22
  25.9 18.8 %collective-permute-start.10 = (bf16[48,2048]{1,0:T(8,128)(2,1)S(1)}, bf16[48,2048]{1,0:T(8,128)(2,1)S(1)}, u32[]{:S(2)}, u32[]{:S(2)}) collective-permute-start(bf16[48,2048]{1,0:T(8,128)(2,1)S(1)} %get-tuple-element.39), channel_id=1, source_target_pairs={{0,12},{1,13},{2,14},{3,15},{4,8},{5,9},{6,10},{7,11},{8,20},{9,21... | collective-permute-start | bytes 589832 | tf_op jit(solution)/shard_map/ppermute | solution.py:22
  30.4 40.2 %collective-permute-start.4 = (bf16[96,2048]{1,0:T(8,128)(2,1)S(1)}, bf16[96,2048]{1,0:T(8,128)(2,1)S(1)}, u32[]{:S(2)}, u32[]{:S(2)}) collective-permute-start(bf16[96,2048]{1,0:T(8,128)(2,1)S(1)} %get-tuple-element.31), channel_id=1, source_target_pairs={{0,24},{1,25},{2,26},{3,27},{4,28},{5,29},{6,30},{7,31},{8,0},{9,1... | collective-permute-start | bytes 1179656 | tf_op jit(solution)/shard_map/ppermute | solution.py:22
  37.7 33.1 %collective-permute-start.13 = (bf16[80,2048]{1,0:T(8,128)(2,1)S(1)}, bf16[80,2048]{1,0:T(8,128)(2,1)S(1)}, u32[]{:S(2)}, u32[]{:S(2)}) collective-permute-start(bf16[80,2048]{1,0:T(8,128)(2,1)S(1)} %get-tuple-element.42), channel_id=1, source_target_pairs={{0,26},{1,27},{2,24},{3,25},{4,30},{5,31},{6,28},{7,29},{8,2},{9,3... | collective-permute-start | bytes 983048 | tf_op jit(solution)/shard_map/ppermute | solution.py:22
  37.7 10.8 %collective-permute-start.8 = (bf16[32,2048]{1,0:T(8,128)(2,1)S(1)}, bf16[32,2048]{1,0:T(8,128)(2,1)S(1)}, u32[]{:S(2)}, u32[]{:S(2)}) collective-permute-start(bf16[32,2048]{1,0:T(8,128)(2,1)S(1)} %get-tuple-element.37.refs_7_), channel_id=1, source_target_pairs={{0,28},{1,29},{2,30},{3,31},{4,24},{5,25},{6,26},{7,27},{8,4},{9,5... | collective-permute-start | bytes 393224 | tf_op jit(solution)/shard_map/ppermute | solution.py:22
  47.1 15.3 %collective-permute-start.11 = (bf16[48,2048]{1,0:T(8,128)(2,1)S(1)}, bf16[48,2048]{1,0:T(8,128)(2,1)S(1)}, u32[]{:S(2)}, u32[]{:S(2)}) collective-permute-start(bf16[48,2048]{1,0:T(8,128)(2,1)S(1)} %get-tuple-element.40), channel_id=1, source_target_pairs={{0,30},{1,31},{2,28},{3,29},{4,26},{5,27},{6,24},{7,25},{8,6},{9,7... | collective-permute-start | bytes 589832 | tf_op jit(solution)/shard_map/ppermute | solution.py:22
  48.3 22.3 %collective-permute-start.12 = (bf16[48,2048]{1,0:T(8,128)(2,1)S(1)}, bf16[48,2048]{1,0:T(8,128)(2,1)S(1)}, u32[]{:S(2)}, u32[]{:S(2)}) collective-permute-start(bf16[48,2048]{1,0:T(8,128)(2,1)S(1)} %get-tuple-element.41), channel_id=1, source_target_pairs={{0,28},{1,29},{2,30},{3,31},{4,24},{5,25},{6,26},{7,27},{8,4},{9,5... | collective-permute-start | bytes 589832 | tf_op jit(solution)/shard_map/ppermute | solution.py:22
  48.6 13.8 %collective-permute-start.5 = (bf16[32,2048]{1,0:T(8,128)(2,1)S(1)}, bf16[32,2048]{1,0:T(8,128)(2,1)S(1)}, u32[]{:S(2)}, u32[]{:S(2)}) collective-permute-start(bf16[32,2048]{1,0:T(8,128)(2,1)S(1)} %get-tuple-element.34.refs_7_), channel_id=1, source_target_pairs={{0,30},{1,31},{2,28},{3,29},{4,26},{5,27},{6,24},{7,25},{8,6},{9,7... | collective-permute-start | bytes 393224 | tf_op jit(solution)/shard_map/ppermute | solution.py:22
  70.6 2.2 %collective-permute-start.14 = (bf16[120,2048]{1,0:T(8,128)(2,1)S(1)}, bf16[120,2048]{1,0:T(8,128)(2,1)S(1)}, u32[]{:S(2)}, u32[]{:S(2)}) collective-permute-start(bf16[120,2048]{1,0:T(8,128)(2,1)S(1)} %stack.2), channel_id=1, source_target_pairs={{0,1},{1,0},{2,3},{3,2},{4,5},{5,4},{6,7},{7,6},{8,9},{9,8},{10,11... | collective-permute-start | bytes 1474568 | tf_op jit(solution)/shard_map/ppermute | solution.py:22
  70.8 2.0 %collective-permute-start.15 = (bf16[40,2048]{1,0:T(8,128)(2,1)S(1)}, bf16[40,2048]{1,0:T(8,128)(2,1)S(1)}, u32[]{:S(2)}, u32[]{:S(2)}) collective-permute-start(bf16[40,2048]{1,0:T(8,128)(2,1)S(1)} %stack.3), channel_id=1, source_target_pairs={{0,1},{1,0},{2,3},{3,2},{4,5},{5,4},{6,7},{7,6},{8,9},{9,8},{10,11... | collective-permute-start | bytes 491528 | tf_op jit(solution)/shard_map/ppermute | solution.py:22
